TPU v7x, 512 devices: a whole 4x8x8 slice. The times are simulated.
512 devices in a mesh: region: 8 (over y), cell: 64 (over z, x, core).
Axes of the slice: x: 4, y: 8, z: 8, core: 2. Of those that a mesh axis runs over, the one named last changes fastest.
Arguments:
- position: float32 [3, 4096, 128], P(None, ('region', 'cell')), may hold values from 0 to 1
- velocity: float32 [3, 4096, 128], P(None, ('region', 'cell')), may hold values from -6 to 6
- smoothing: float32 [4096, 128], P(('region', 'cell')), may hold values from 0.3 to 0.5
- particle_mass: float32 [4096, 128], P(('region', 'cell')), may hold values from 0.004 to 0.012
- energy: float32 [4096, 128], P(('region', 'cell')), may hold values from 0.5 to 2
- density_old: float32 [4096, 128], P(('region', 'cell')), may hold values from 0.3 to 1.2
- cell_count: int32 [4096], P(('region', 'cell')), may hold values from 8 to 128, as said below
- active: int32 [4096, 128], P(('region', 'cell')), may hold values from 0 to 1, as said below
- time_bin: int32 [4096, 128], P(('region', 'cell')), may hold values from 0 to 5
- pair_source: int32 [4096, 27], P(('region', 'cell')), may hold values from 0 to 137, as said below
- pair_shift: int32 [4096, 27], P(('region', 'cell')), may hold values from 0 to 26, as said below
- export: int32 [32768, 2], P(('region', 'cell')), may hold values from 0 to 7
Outputs:
- density: float32 [4096, 128], P(('region', 'cell'))
- acceleration: float32 [3, 4096, 128], P(None, ('region', 'cell'))
- kicked_velocity: float32 [3, 4096, 128], P(None, ('region', 'cell'))
Inputs may be any that keep to these rules, and one draw needn't show every extreme that they name: `cell_count`: every device has a cell of exactly 128 particles. `active`: 0 in the slots past a cell's count. `pair_source`: pair 0 of a device's cell k names source k; a device's pairs name every one of its 138 sources. `pair_shift`: pair 0 has code 13; a cell's 27 codes are distinct.
All inputs are finite; a program needn't handle non-finite values.
Results may differ from a plain program's by a relative error of at most 0.0003.
Values sent between devices are 32-bit elements; how exact they have to be, the bound alone decides.
A program may use at most 64 MiB of HBM per device.

v0:
```python
import math

import jax
import jax.numpy as jnp
from jax import lax
from jax.sharding import PartitionSpec as P

ADIABATIC = 5.0 / 3.0
VISC_ALPHA = 1.0
VISC_BETA = 2.0
STEP_MAX = 0.2


def extended(x, sides, width):
    for axis, dim in sides:
        size, length = (lax.axis_size(axis), x.shape[dim])
        up = [(i, (i + 1) % size) for i in range(size)]
        down = [(j, i) for i, j in up]
        last = lax.slice_in_dim(x, length - width, length, axis=dim)
        leading = lax.slice_in_dim(x, 0, width, axis=dim)
        before = lax.ppermute(last, axis, up)
        after = lax.ppermute(leading, axis, down)
        x = jnp.concatenate([before, x, after], axis=dim)
    return x


def kernel_value(radius, smooth):
    scaled = radius / smooth
    factor = 1.0 / (math.pi * smooth * smooth * smooth)
    inner_part = 1.0 - 1.5 * scaled * scaled + 0.75 * scaled * scaled * scaled
    outer_part = 0.25 * jnp.maximum(2.0 - scaled, 0.0) ** 3
    return factor * jnp.where(scaled < 1.0, inner_part, outer_part)


def kernel_slope(radius, smooth):
    scaled = radius / smooth
    factor = 1.0 / (math.pi * smooth * smooth * smooth * smooth * smooth)
    inner_part = -3.0 + 2.25 * scaled
    bounded = jnp.maximum(scaled, 1.0)
    outer_part = -0.75 * jnp.maximum(2.0 - bounded, 0.0) ** 2 / bounded
    return factor * jnp.where(scaled < 1.0, inner_part, outer_part)


def shift_offsets(shift_codes):
    first = shift_codes // 9 - 1
    second = shift_codes // 3 % 3 - 1
    third = shift_codes % 3 - 1
    return jnp.stack([first, second, third], axis=-1).astype(jnp.float32)


def density_terms(target_pos, target_smooth, source_pos, source_mass):
    square = sum(((target_pos[component] - source_pos[component]) ** 2 for component in range(3)))
    radius = jnp.sqrt(square)
    return source_mass * kernel_value(radius, target_smooth)


def force_terms(
    target_pos,
    target_vel,
    target_smooth,
    target_press,
    target_sound,
    target_dens,
    source_pos,
    source_vel,
    source_smooth,
    source_mass,
    source_press,
    source_sound,
    source_dens,
):
    separation = [target_pos[component] - source_pos[component] for component in range(3)]
    square = sum((piece * piece for piece in separation))
    radius = jnp.sqrt(square)
    mean_slope = 0.5 * (kernel_slope(radius, target_smooth) + kernel_slope(radius, source_smooth))
    approach = sum(
        (
            (target_vel[component] - source_vel[component]) * separation[component]
            for component in range(3)
        )
    )
    mean_smooth = 0.5 * (target_smooth + source_smooth)
    mu_term = mean_smooth * jnp.minimum(approach, 0.0) / (square + 0.01 * mean_smooth * mean_smooth)
    viscous = (
        -VISC_ALPHA * 0.5 * (target_sound + source_sound) * mu_term + VISC_BETA * mu_term * mu_term
    ) / (0.5 * (target_dens + source_dens))
    weight = source_mass * (target_press + source_press + viscous) * mean_slope
    return [-weight * piece for piece in separation]


def import_cells(stacked, export):
    outgoing = stacked[export]
    incoming = lax.all_to_all(outgoing, "cell", split_axis=0, concat_axis=0, tiled=True)
    bordered = extended(stacked, (("region", 0),), 1)
    received = incoming.reshape((-1,) + stacked.shape[1:])
    return jnp.concatenate([stacked, received, bordered[:1], bordered[-1:]], axis=0)


def shards(
    position,
    velocity,
    smoothing,
    particle_mass,
    energy,
    density_old,
    cell_count,
    active,
    time_bin,
    pair_source,
    pair_shift,
    export,
):
    cells, capacity = smoothing.shape
    slot_index = lax.broadcasted_iota(jnp.int32, (cells, capacity), 1)
    live_slot = slot_index < cell_count[:, None]
    mass_live = jnp.where(live_slot, particle_mass, 0.0)
    is_active = active > 0
    offsets = jnp.moveaxis(shift_offsets(pair_shift), 1, 0)
    static_rows = [position[0], position[1], position[2], mass_live]
    moving_rows = [smoothing, energy, velocity[0], velocity[1], velocity[2]]
    table_one = import_cells(jnp.stack(static_rows, axis=1), export)
    gathered = jnp.moveaxis(table_one[pair_source], 1, 0)
    target_pos = [position[component][:, :, None] for component in range(3)]
    target_smooth = smoothing[:, :, None]

    def add_density(total, pieces):
        source, shift = pieces
        source_pos = [
            source[:, component, None, :] + shift[:, component, None, None]
            for component in range(3)
        ]
        pair_terms = density_terms(target_pos, target_smooth, source_pos, source[:, 3, None, :])
        return (total + jnp.sum(pair_terms, axis=2), None)

    summed = lax.scan(add_density, jnp.zeros((cells, capacity), jnp.float32), (gathered, offsets))[
        0
    ]
    density = jnp.where(is_active, summed, density_old)
    press_term = (ADIABATIC - 1.0) * energy / density
    sound_speed = jnp.sqrt(ADIABATIC * (ADIABATIC - 1.0) * energy)
    second_rows = moving_rows + [density]
    table_two = import_cells(jnp.stack(second_rows, axis=1), export)
    full_table = jnp.concatenate([table_one, table_two], axis=1)
    gathered_all = jnp.moveaxis(full_table[pair_source], 1, 0)
    target_vel = [velocity[component][:, :, None] for component in range(3)]
    target_press = press_term[:, :, None]
    target_sound = sound_speed[:, :, None]
    target_dens = density[:, :, None]

    def add_force(total, pieces):
        source, shift = pieces
        source_pos = [
            source[:, component, None, :] + shift[:, component, None, None]
            for component in range(3)
        ]
        source_vel = [source[:, 6 + component, None, :] for component in range(3)]
        source_energy = source[:, 5, None, :]
        source_dens = source[:, 9, None, :]
        source_press = (ADIABATIC - 1.0) * source_energy / source_dens
        source_sound = jnp.sqrt(ADIABATIC * (ADIABATIC - 1.0) * source_energy)
        pair_terms = force_terms(
            target_pos,
            target_vel,
            target_smooth,
            target_press,
            target_sound,
            target_dens,
            source_pos,
            source_vel,
            source[:, 4, None, :],
            source[:, 3, None, :],
            source_press,
            source_sound,
            source_dens,
        )
        return (total + jnp.stack([jnp.sum(piece, axis=2) for piece in pair_terms], axis=0), None)

    accel_cells = lax.scan(
        add_force, jnp.zeros((3, cells, capacity), jnp.float32), (gathered_all, offsets)
    )[0]
    acceleration = jnp.where(is_active[None], accel_cells, 0.0)
    step_size = STEP_MAX * jnp.exp2(-time_bin.astype(jnp.float32))
    kicked_velocity = velocity + acceleration * step_size[None]
    return (density, acceleration, kicked_velocity)


def solution(mesh):
    placed = (
        P(None, ("region", "cell"), None),
        P(None, ("region", "cell"), None),
        P(("region", "cell"), None),
        P(("region", "cell"), None),
        P(("region", "cell"), None),
        P(("region", "cell"), None),
        P(("region", "cell")),
        P(("region", "cell"), None),
        P(("region", "cell"), None),
        P(("region", "cell"), None),
        P(("region", "cell"), None),
        P(("region", "cell"), None),
    )
    return jax.shard_map(
        shards,
        mesh=mesh,
        in_specs=placed,
        out_specs=(
            P(("region", "cell"), None),
            P(None, ("region", "cell"), None),
            P(None, ("region", "cell"), None),
        ),
        check_vma=False,
    )
```

profile of v0, /device:TPU:57, one launch (start us, length us, event | category | flops | bytes accessed | tf_op | source)
XLA Modules:
  0.0 165.7 jit_solution(13677984389886508715)
XLA Ops:
  4.6 14.1 %all-to-all-start = ((f32[64,2,4,128]{3,2,1,0:T(4,128)}), f32[64,2,4,128]{3,2,1,0:T(4,128)S(1)}, u32[]{:S(2)}, u32[]{:S(2)}) async-start(f32[64,2,4,128]{3,2,1,0:T(4,128)} %bitcast.4), calls=%async_computation | async-start | bytes 524288 | tf_op jit(solution)/shard_map/all_to_all | solution.py:93
  20.7 3.4 %collective-permute-start.1 = (f32[1,4,128]{2,1,0:T(4,128)S(1)}, f32[1,4,128]{2,1,0:T(4,128)S(1)}, u32[]{:S(2)}, u32[]{:S(2)}) collective-permute-start(f32[1,4,128]{2,1,0:T(4,128)S(1)} %get-tuple-element.449), channel_id=1, source_target_pairs={{64,0},{128,64},{192,128},{256,192},{320,256},{384,320},{448,384},... | collective-permute-start | bytes 6152 | tf_op jit(solution)/shard_map/ppermute | solution.py:22
  26.5 5.4 %all-to-all-done = f32[64,2,4,128]{3,2,1,0:T(4,128)S(1)} async-done(((f32[64,2,4,128]{3,2,1,0:T(4,128)}), f32[64,2,4,128]{3,2,1,0:T(4,128)S(1)}, u32[]{:S(2)}, u32[]{:S(2)}) %all-to-all-start) | async-done | bytes 262176 | tf_op jit(solution)/shard_map/all_to_all | solution.py:93
  33.0 34.2 %while.24 = (s32[]{:T(128)}, f32[8,128]{1,0:T(8,128)S(1)}, f32[27,8,4,128]{3,2,0,1:T(4,128)S(1)}, f32[8,128,1]{1,0,2:T(8,128)S(1)}, f32[8,128,1]{1,0,2:T(8,128)S...) while((s32[]{:T(128)}, f32[8,128]{1,0:T(8,128)S(1)}, ...), condition=%wide.region_2.3_spmd.clone, body=%wide.region_0.2_spmd.clone.sunk | while | flops 3416067 | bytes 160343 | solution.py:135
  69.0 5.8 %all-to-all-start.1 = ((f32[64,2,6,128]{3,1,2,0:T(2,128)}), f32[64,2,6,128]{3,1,2,0:T(2,128)S(1)}, u32[]{:S(2)}, u32[]{:S(2)}) async-start(f32[64,2,6,128]{3,1,2,0:T(2,128)} %copy.70), calls=%async_computation.1 | async-start | bytes 786432 | tf_op jit(solution)/shard_map/all_to_all | solution.py:93
  76.7 3.4 %collective-permute-start.3 = (f32[1,6,128]{2,1,0:T(8,128)S(1)}, f32[1,6,128]{2,1,0:T(8,128)S(1)}, u32[]{:S(2)}, u32[]{:S(2)}) collective-permute-start(f32[1,6,128]{2,1,0:T(8,128)S(1)} %get-tuple-element.447), channel_id=1, source_target_pairs={{64,0},{128,64},{192,128},{256,192},{320,256},{384,320},{448,384},... | collective-permute-start | bytes 9224 | tf_op jit(solution)/shard_map/ppermute | solution.py:22
  80.1 9.7 %all-to-all-done.1 = f32[64,2,6,128]{3,1,2,0:T(2,128)S(1)} async-done(((f32[64,2,6,128]{3,1,2,0:T(2,128)}), f32[64,2,6,128]{3,1,2,0:T(2,128)S(1)}, u32[]{:S(2)}, u32[]{:S(2)}) %all-to-all-start.1) | async-done | bytes 393248 | tf_op jit(solution)/shard_map/all_to_all | solution.py:93
  91.5 73.5 %while.25 = (s32[]{:T(128)}, f32[3,8,128]{2,1,0:T(8,128)S(1)}, f32[27,8,10,128]{3,1,2,0:T(8,128)S(1)}, f32[8,128,1]{1,0,2:T(8,128)S(1)}, f32[8,128,1]{1,0,2:T(8,...) while((s32[]{:T(128)}, f32[3,8,128]{2,1,0:T(8,128)S(1)}, ...), condition=%wide.region_7.8_spmd.clone, body=%wide.region_3.7_spmd.clone.sunk | while | flops 9071619 | bytes 324231 | solution.py:178
  91.7 2.5 %fusion.53 = (f32[8,128]{1,0:T(8,128)S(1)}, f32[8,128]{1,0:T(8,128)S(1)}, f32[8,128]{1,0:T(8,128)S(1)}) fusion(f32[8,128]{1,0:T(8,128)S(1)} %get-tuple-element.641, f32[8,128]{1,0:T(8,128)S(1)} %bitcast.213, f32[8,128]{1,0:T(8,128)S(1)} %get-tuple-element.642, f32[8,128]{1,0:T(8,128)S(1)} %bitcast.215, f32[8,128]{1,0:T(8,128)S(1)} %get-tuple-element.643, ...), kind=kLoop, calls=%fused_computation.51.clone.1 | loop fusion | flops 9040896 | bytes 106496 | tf_op jit(solution)/shard_map/while/body/eval_jaxpr/reduce_sum | solution.py:176
  94.4 2.5 %fusion.53 = (f32[8,128]{1,0:T(8,128)S(1)}, f32[8,128]{1,0:T(8,128)S(1)}, f32[8,128]{1,0:T(8,128)S(1)}) fusion(f32[8,128]{1,0:T(8,128)S(1)} %get-tuple-element.641, f32[8,128]{1,0:T(8,128)S(1)} %bitcast.213, f32[8,128]{1,0:T(8,128)S(1)} %get-tuple-element.642, f32[8,128]{1,0:T(8,128)S(1)} %bitcast.215, f32[8,128]{1,0:T(8,128)S(1)} %get-tuple-element.643, ...), kind=kLoop, calls=%fused_computation.51.clone.1 | loop fusion | flops 9040896 | bytes 106496 | tf_op jit(solution)/shard_map/while/body/eval_jaxpr/reduce_sum | solution.py:176
  99.8 2.5 %fusion.53 = (f32[8,128]{1,0:T(8,128)S(1)}, f32[8,128]{1,0:T(8,128)S(1)}, f32[8,128]{1,0:T(8,128)S(1)}) fusion(f32[8,128]{1,0:T(8,128)S(1)} %get-tuple-element.641, f32[8,128]{1,0:T(8,128)S(1)} %bitcast.213, f32[8,128]{1,0:T(8,128)S(1)} %get-tuple-element.642, f32[8,128]{1,0:T(8,128)S(1)} %bitcast.215, f32[8,128]{1,0:T(8,128)S(1)} %get-tuple-element.643, ...), kind=kLoop, calls=%fused_computation.51.clone.1 | loop fusion | flops 9040896 | bytes 106496 | tf_op jit(solution)/shard_map/while/body/eval_jaxpr/reduce_sum | solution.py:176
  102.6 2.5 %fusion.53 = (f32[8,128]{1,0:T(8,128)S(1)}, f32[8,128]{1,0:T(8,128)S(1)}, f32[8,128]{1,0:T(8,128)S(1)}) fusion(f32[8,128]{1,0:T(8,128)S(1)} %get-tuple-element.641, f32[8,128]{1,0:T(8,128)S(1)} %bitcast.213, f32[8,128]{1,0:T(8,128)S(1)} %get-tuple-element.642, f32[8,128]{1,0:T(8,128)S(1)} %bitcast.215, f32[8,128]{1,0:T(8,128)S(1)} %get-tuple-element.643, ...), kind=kLoop, calls=%fused_computation.51.clone.1 | loop fusion | flops 9040896 | bytes 106496 | tf_op jit(solution)/shard_map/while/body/eval_jaxpr/reduce_sum | solution.py:176
  108.0 2.5 %fusion.53 = (f32[8,128]{1,0:T(8,128)S(1)}, f32[8,128]{1,0:T(8,128)S(1)}, f32[8,128]{1,0:T(8,128)S(1)}) fusion(f32[8,128]{1,0:T(8,128)S(1)} %get-tuple-element.641, f32[8,128]{1,0:T(8,128)S(1)} %bitcast.213, f32[8,128]{1,0:T(8,128)S(1)} %get-tuple-element.642, f32[8,128]{1,0:T(8,128)S(1)} %bitcast.215, f32[8,128]{1,0:T(8,128)S(1)} %get-tuple-element.643, ...), kind=kLoop, calls=%fused_computation.51.clone.1 | loop fusion | flops 9040896 | bytes 106496 | tf_op jit(solution)/shard_map/while/body/eval_jaxpr/reduce_sum | solution.py:176
  110.7 2.5 %fusion.53 = (f32[8,128]{1,0:T(8,128)S(1)}, f32[8,128]{1,0:T(8,128)S(1)}, f32[8,128]{1,0:T(8,128)S(1)}) fusion(f32[8,128]{1,0:T(8,128)S(1)} %get-tuple-element.641, f32[8,128]{1,0:T(8,128)S(1)} %bitcast.213, f32[8,128]{1,0:T(8,128)S(1)} %get-tuple-element.642, f32[8,128]{1,0:T(8,128)S(1)} %bitcast.215, f32[8,128]{1,0:T(8,128)S(1)} %get-tuple-element.643, ...), kind=kLoop, calls=%fused_computation.51.clone.1 | loop fusion | flops 9040896 | bytes 106496 | tf_op jit(solution)/shard_map/while/body/eval_jaxpr/reduce_sum | solution.py:176
  113.5 2.5 %fusion.53 = (f32[8,128]{1,0:T(8,128)S(1)}, f32[8,128]{1,0:T(8,128)S(1)}, f32[8,128]{1,0:T(8,128)S(1)}) fusion(f32[8,128]{1,0:T(8,128)S(1)} %get-tuple-element.641, f32[8,128]{1,0:T(8,128)S(1)} %bitcast.213, f32[8,128]{1,0:T(8,128)S(1)} %get-tuple-element.642, f32[8,128]{1,0:T(8,128)S(1)} %bitcast.215, f32[8,128]{1,0:T(8,128)S(1)} %get-tuple-element.643, ...), kind=kLoop, calls=%fused_computation.51.clone.1 | loop fusion | flops 9040896 | bytes 106496 | tf_op jit(solution)/shard_map/while/body/eval_jaxpr/reduce_sum | solution.py:176
  116.2 2.5 %fusion.53 = (f32[8,128]{1,0:T(8,128)S(1)}, f32[8,128]{1,0:T(8,128)S(1)}, f32[8,128]{1,0:T(8,128)S(1)}) fusion(f32[8,128]{1,0:T(8,128)S(1)} %get-tuple-element.641, f32[8,128]{1,0:T(8,128)S(1)} %bitcast.213, f32[8,128]{1,0:T(8,128)S(1)} %get-tuple-element.642, f32[8,128]{1,0:T(8,128)S(1)} %bitcast.215, f32[8,128]{1,0:T(8,128)S(1)} %get-tuple-element.643, ...), kind=kLoop, calls=%fused_computation.51.clone.1 | loop fusion | flops 9040896 | bytes 106496 | tf_op jit(solution)/shard_map/while/body/eval_jaxpr/reduce_sum | solution.py:176
  121.6 2.5 %fusion.53 = (f32[8,128]{1,0:T(8,128)S(1)}, f32[8,128]{1,0:T(8,128)S(1)}, f32[8,128]{1,0:T(8,128)S(1)}) fusion(f32[8,128]{1,0:T(8,128)S(1)} %get-tuple-element.641, f32[8,128]{1,0:T(8,128)S(1)} %bitcast.213, f32[8,128]{1,0:T(8,128)S(1)} %get-tuple-element.642, f32[8,128]{1,0:T(8,128)S(1)} %bitcast.215, f32[8,128]{1,0:T(8,128)S(1)} %get-tuple-element.643, ...), kind=kLoop, calls=%fused_computation.51.clone.1 | loop fusion | flops 9040896 | bytes 106496 | tf_op jit(solution)/shard_map/while/body/eval_jaxpr/reduce_sum | solution.py:176
  124.3 2.5 %fusion.53 = (f32[8,128]{1,0:T(8,128)S(1)}, f32[8,128]{1,0:T(8,128)S(1)}, f32[8,128]{1,0:T(8,128)S(1)}) fusion(f32[8,128]{1,0:T(8,128)S(1)} %get-tuple-element.641, f32[8,128]{1,0:T(8,128)S(1)} %bitcast.213, f32[8,128]{1,0:T(8,128)S(1)} %get-tuple-element.642, f32[8,128]{1,0:T(8,128)S(1)} %bitcast.215, f32[8,128]{1,0:T(8,128)S(1)} %get-tuple-element.643, ...), kind=kLoop, calls=%fused_computation.51.clone.1 | loop fusion | flops 9040896 | bytes 106496 | tf_op jit(solution)/shard_map/while/body/eval_jaxpr/reduce_sum | solution.py:176
  129.8 2.5 %fusion.53 = (f32[8,128]{1,0:T(8,128)S(1)}, f32[8,128]{1,0:T(8,128)S(1)}, f32[8,128]{1,0:T(8,128)S(1)}) fusion(f32[8,128]{1,0:T(8,128)S(1)} %get-tuple-element.641, f32[8,128]{1,0:T(8,128)S(1)} %bitcast.213, f32[8,128]{1,0:T(8,128)S(1)} %get-tuple-element.642, f32[8,128]{1,0:T(8,128)S(1)} %bitcast.215, f32[8,128]{1,0:T(8,128)S(1)} %get-tuple-element.643, ...), kind=kLoop, calls=%fused_computation.51.clone.1 | loop fusion | flops 9040896 | bytes 106496 | tf_op jit(solution)/shard_map/while/body/eval_jaxpr/reduce_sum | solution.py:176
  132.5 2.5 %fusion.53 = (f32[8,128]{1,0:T(8,128)S(1)}, f32[8,128]{1,0:T(8,128)S(1)}, f32[8,128]{1,0:T(8,128)S(1)}) fusion(f32[8,128]{1,0:T(8,128)S(1)} %get-tuple-element.641, f32[8,128]{1,0:T(8,128)S(1)} %bitcast.213, f32[8,128]{1,0:T(8,128)S(1)} %get-tuple-element.642, f32[8,128]{1,0:T(8,128)S(1)} %bitcast.215, f32[8,128]{1,0:T(8,128)S(1)} %get-tuple-element.643, ...), kind=kLoop, calls=%fused_computation.51.clone.1 | loop fusion | flops 9040896 | bytes 106496 | tf_op jit(solution)/shard_map/while/body/eval_jaxpr/reduce_sum | solution.py:176
  135.2 2.5 %fusion.53 = (f32[8,128]{1,0:T(8,128)S(1)}, f32[8,128]{1,0:T(8,128)S(1)}, f32[8,128]{1,0:T(8,128)S(1)}) fusion(f32[8,128]{1,0:T(8,128)S(1)} %get-tuple-element.641, f32[8,128]{1,0:T(8,128)S(1)} %bitcast.213, f32[8,128]{1,0:T(8,128)S(1)} %get-tuple-element.642, f32[8,128]{1,0:T(8,128)S(1)} %bitcast.215, f32[8,128]{1,0:T(8,128)S(1)} %get-tuple-element.643, ...), kind=kLoop, calls=%fused_computation.51.clone.1 | loop fusion | flops 9040896 | bytes 106496 | tf_op jit(solution)/shard_map/while/body/eval_jaxpr/reduce_sum | solution.py:176
  137.9 2.5 %fusion.53 = (f32[8,128]{1,0:T(8,128)S(1)}, f32[8,128]{1,0:T(8,128)S(1)}, f32[8,128]{1,0:T(8,128)S(1)}) fusion(f32[8,128]{1,0:T(8,128)S(1)} %get-tuple-element.641, f32[8,128]{1,0:T(8,128)S(1)} %bitcast.213, f32[8,128]{1,0:T(8,128)S(1)} %get-tuple-element.642, f32[8,128]{1,0:T(8,128)S(1)} %bitcast.215, f32[8,128]{1,0:T(8,128)S(1)} %get-tuple-element.643, ...), kind=kLoop, calls=%fused_computation.51.clone.1 | loop fusion | flops 9040896 | bytes 106496 | tf_op jit(solution)/shard_map/while/body/eval_jaxpr/reduce_sum | solution.py:176
  140.7 2.5 %fusion.53 = (f32[8,128]{1,0:T(8,128)S(1)}, f32[8,128]{1,0:T(8,128)S(1)}, f32[8,128]{1,0:T(8,128)S(1)}) fusion(f32[8,128]{1,0:T(8,128)S(1)} %get-tuple-element.641, f32[8,128]{1,0:T(8,128)S(1)} %bitcast.213, f32[8,128]{1,0:T(8,128)S(1)} %get-tuple-element.642, f32[8,128]{1,0:T(8,128)S(1)} %bitcast.215, f32[8,128]{1,0:T(8,128)S(1)} %get-tuple-element.643, ...), kind=kLoop, calls=%fused_computation.51.clone.1 | loop fusion | flops 9040896 | bytes 106496 | tf_op jit(solution)/shard_map/while/body/eval_jaxpr/reduce_sum | solution.py:176
  143.4 2.5 %fusion.53 = (f32[8,128]{1,0:T(8,128)S(1)}, f32[8,128]{1,0:T(8,128)S(1)}, f32[8,128]{1,0:T(8,128)S(1)}) fusion(f32[8,128]{1,0:T(8,128)S(1)} %get-tuple-element.641, f32[8,128]{1,0:T(8,128)S(1)} %bitcast.213, f32[8,128]{1,0:T(8,128)S(1)} %get-tuple-element.642, f32[8,128]{1,0:T(8,128)S(1)} %bitcast.215, f32[8,128]{1,0:T(8,128)S(1)} %get-tuple-element.643, ...), kind=kLoop, calls=%fused_computation.51.clone.1 | loop fusion | flops 9040896 | bytes 106496 | tf_op jit(solution)/shard_map/while/body/eval_jaxpr/reduce_sum | solution.py:176
  (443 shorter events, 78.8 us)
Async XLA Ops:
  0.6 23.4 %copy-start.4 = (s32[8,27]{1,0:T(8,128)S(1)}, s32[8,27]{1,0:T(8,128)}, u32[]{:S(2)}) copy-start(s32[8,27]{1,0:T(8,128)} %param.25) | copy-start | bytes 2596
  0.6 23.5 %copy-start.6 = (s32[8,27]{1,0:T(8,128)S(1)}, s32[8,27]{1,0:T(8,128)}, u32[]{:S(2)}) copy-start(s32[8,27]{1,0:T(8,128)} %param.26) | copy-start | bytes 2596
  4.6 28.3 %copy-start = (f32[8,128]{1,0:T(8,128)S(1)}, f32[8,128]{1,0:T(8,128)}, u32[]{:S(2)}) copy-start(f32[8,128]{1,0:T(8,128)} %param.18) | copy-start | bytes 12292
  4.6 27.3 %all-to-all-start = ((f32[64,2,4,128]{3,2,1,0:T(4,128)}), f32[64,2,4,128]{3,2,1,0:T(4,128)S(1)}, u32[]{:S(2)}, u32[]{:S(2)}) async-start(f32[64,2,4,128]{3,2,1,0:T(4,128)} %bitcast.4), calls=%async_computation | async-start | bytes 524288 | tf_op jit(solution)/shard_map/all_to_all | solution.py:93
  18.8 5.6 %collective-permute-start = (f32[1,4,128]{2,1,0:T(4,128)S(1)}, f32[1,4,128]{2,1,0:T(4,128)S(1)}, u32[]{:S(2)}, u32[]{:S(2)}) collective-permute-start(f32[1,4,128]{2,1,0:T(4,128)S(1)} %get-tuple-element.448), channel_id=1, source_target_pairs={{0,64},{64,128},{128,192},{192,256},{256,320},{320,384},{384,448},... | collective-permute-start | bytes 6152 | tf_op jit(solution)/shard_map/ppermute | solution.py:21
  20.7 5.8 %collective-permute-start.1 = (f32[1,4,128]{2,1,0:T(4,128)S(1)}, f32[1,4,128]{2,1,0:T(4,128)S(1)}, u32[]{:S(2)}, u32[]{:S(2)}) collective-permute-start(f32[1,4,128]{2,1,0:T(4,128)S(1)} %get-tuple-element.449), channel_id=1, source_target_pairs={{64,0},{128,64},{192,128},{256,192},{320,256},{384,320},{448,384},... | collective-permute-start | bytes 6152 | tf_op jit(solution)/shard_map/ppermute | solution.py:22
  32.9 34.2 %copy-start.2 = (f32[8,128]{1,0:T(8,128)S(1)}, f32[8,128]{1,0:T(8,128)}, u32[]{:S(2)}) copy-start(f32[8,128]{1,0:T(8,128)} %param.20) | copy-start | bytes 12292
  32.9 34.2 %copy-start.7 = (f32[8,128]{1,0:T(8,128)S(1)}, f32[8,128]{1,0:T(8,128)}, u32[]{:S(2)}) copy-start(f32[8,128]{1,0:T(8,128)} %param.21) | copy-start | bytes 12292
  32.9 34.2 %copy-start.8 = (s32[8,128]{1,0:T(8,128)S(1)}, s32[8,128]{1,0:T(8,128)}, u32[]{:S(2)}) copy-start(s32[8,128]{1,0:T(8,128)} %param.23) | copy-start | bytes 12292
  68.0 12.1 %copy-start.5 = (s32[8,128]{1,0:T(8,128)S(1)}, s32[8,128]{1,0:T(8,128)}, u32[]{:S(2)}) copy-start(s32[8,128]{1,0:T(8,128)} %param.24) | copy-start | bytes 12292
  69.0 20.8 %all-to-all-start.1 = ((f32[64,2,6,128]{3,1,2,0:T(2,128)}), f32[64,2,6,128]{3,1,2,0:T(2,128)S(1)}, u32[]{:S(2)}, u32[]{:S(2)}) async-start(f32[64,2,6,128]{3,1,2,0:T(2,128)} %copy.70), calls=%async_computation.1 | async-start | bytes 786432 | tf_op jit(solution)/shard_map/all_to_all | solution.py:93
  74.8 15.1 %collective-permute-start.2 = (f32[1,6,128]{2,1,0:T(8,128)S(1)}, f32[1,6,128]{2,1,0:T(8,128)S(1)}, u32[]{:S(2)}, u32[]{:S(2)}) collective-permute-start(f32[1,6,128]{2,1,0:T(8,128)S(1)} %get-tuple-element.446), channel_id=1, source_target_pairs={{0,64},{64,128},{128,192},{192,256},{256,320},{320,384},{384,448},... | collective-permute-start | bytes 9224 | tf_op jit(solution)/shard_map/ppermute | solution.py:21
  76.7 13.2 %collective-permute-start.3 = (f32[1,6,128]{2,1,0:T(8,128)S(1)}, f32[1,6,128]{2,1,0:T(8,128)S(1)}, u32[]{:S(2)}, u32[]{:S(2)}) collective-permute-start(f32[1,6,128]{2,1,0:T(8,128)S(1)} %get-tuple-element.447), channel_id=1, source_target_pairs={{64,0},{128,64},{192,128},{256,192},{320,256},{384,320},{448,384},... | collective-permute-start | bytes 9224 | tf_op jit(solution)/shard_map/ppermute | solution.py:22
  91.5 73.5 %copy-start.1 = (f32[3,8,128]{2,1,0:T(8,128)S(1)}, f32[3,8,128]{2,1,0:T(8,128)}, u32[]{:S(2)}) copy-start(f32[3,8,128]{2,1,0:T(8,128)} %param.17) | copy-start | bytes 36868
  165.0 0.6 copy-start.3
where the time goes:
time: 169 us; the launch traced here: 166 us
  other arithmetic  105 us (62%)
  starting transfers between devices  30.5 us (18%)
  waiting for transfers between devices  17.3 us (10%)
  local copies, waits for them, and re-layouts  8.25 us (5%)
  loops' own time  3.38 us (2%)
    reduce_sum x27, other arithmetic, add_force(): jnp.sum(piece, axis=2)  68.8 us
    reduce_sum x27, other arithmetic, add_density(): return (total + jnp.sum(pair_terms, axis=2), None)  29.3 us
    all_to_all x2, starting transfers between devices, import_cells(): lax.all_to_all(outgoing, 'cell', split_axis=0, concat_axis=0, tiled=True)  19.9 us
    all_to_all x2, waiting for transfers between devices, import_cells(): lax.all_to_all(outgoing, 'cell', split_axis=0, concat_axis=0, tiled=True)  15.1 us
    ppermute x2, starting transfers between devices, extended(): after = lax.ppermute(leading, axis, down)  6.72 us
    ppermute x2, starting transfers between devices, extended(): before = lax.ppermute(last, axis, up)  3.84 us
  transfers between devices with their start and end apart: 6, of which 3 were waited for; matrix products, arithmetic and copies ran while one was open for 0% of the time, Pallas kernels for 0%

commit v1 on v0

v1 whole, which is shorter than its diff:
```python
import functools
import math

import jax
import jax.numpy as jnp
from jax import lax
from jax.experimental import pallas as pl
from jax.experimental.pallas import tpu as pltpu
from jax.sharding import PartitionSpec as P

MESH = pl.DeviceIdType.MESH
C_DEV = 8
CAP = 128
NB = 27
GROUP = 8
ADIABATIC = 5.0 / 3.0
STEP_MAX = 0.2
TINY = 1e-30
F32 = jnp.float32


def greet(regions, peers):
    r, c = lax.axis_index("region"), lax.axis_index("cell")
    barrier = pltpu.get_barrier_semaphore()

    def signal(i, carry):
        pl.semaphore_signal(
            barrier, inc=1, device_id=(r, lax.rem(c + i, peers)), device_id_type=MESH
        )
        return carry

    lax.fori_loop(1, peers, signal, 0)
    for step in (1, regions - 1):
        pl.semaphore_signal(
            barrier, inc=1, device_id=(lax.rem(r + step, regions), c), device_id_type=MESH
        )
    pl.semaphore_wait(barrier, peers + 1)


def fill_outbox(peers, export, cells, outbox):
    def fill(d, carry):
        for q in range(2):
            outbox[d, q] = cells[export[d, q]]
        return carry

    lax.fori_loop(0, peers, fill, 0, unroll=4)


def region_copies(regions, cells, table, sems):
    r, c = lax.axis_index("region"), lax.axis_index("cell")
    size = table.shape[0]
    up = pltpu.make_async_remote_copy(
        src_ref=cells.at[pl.ds(C_DEV - 1, 1)],
        dst_ref=table.at[pl.ds(size - 2, 1)],
        send_sem=sems.at[2],
        recv_sem=sems.at[3],
        device_id=(lax.rem(r + 1, regions), c),
        device_id_type=MESH,
    )
    down = pltpu.make_async_remote_copy(
        src_ref=cells.at[pl.ds(0, 1)],
        dst_ref=table.at[pl.ds(size - 1, 1)],
        send_sem=sems.at[4],
        recv_sem=sems.at[5],
        device_id=(lax.rem(r + regions - 1, regions), c),
        device_id_type=MESH,
    )
    return up, down


def start_exchange(regions, peers, cells, outbox, table, sems):
    r, c = lax.axis_index("region"), lax.axis_index("cell")
    for copy in region_copies(regions, cells, table, sems):
        copy.start()

    def send(i, carry):
        d = lax.rem(c + i, peers)
        pltpu.make_async_remote_copy(
            src_ref=outbox.at[d],
            dst_ref=table.at[pl.ds(C_DEV + 2 * c, 2)],
            send_sem=sems.at[0],
            recv_sem=sems.at[1],
            device_id=(r, d),
            device_id_type=MESH,
        ).start()
        return carry

    lax.fori_loop(1, peers, send, 0)
    for k in range(C_DEV):
        table[k] = cells[k]
    for q in range(2):
        table[C_DEV + 2 * c + q] = outbox[c, q]


def finish_exchange(regions, peers, cells, outbox, table, sems):
    for copy in region_copies(regions, cells, table, sems):
        copy.wait()
    sent = outbox.at[pl.ds(0, peers - 1)]
    pltpu.make_async_copy(sent, sent, sems.at[0]).wait()
    landed = table.at[pl.ds(0, 2 * (peers - 1))]
    pltpu.make_async_copy(landed, landed, sems.at[1]).wait()


def static_kernel(
    regions, peers,
    export, count, position, velocity, smoothing, mass, energy, active,
    table, comp, rank, groups,
    cells, outbox, sems,
):
    slot = lax.broadcasted_iota(jnp.int32, (1, CAP), 1)
    for k in range(C_DEV):
        for i in range(3):
            cells[k, i : i + 1] = position[i, k : k + 1]
            cells[k, 5 + i : 6 + i] = velocity[i, k : k + 1]
        cells[k, 3:4] = jnp.where(slot < count[k], mass[k : k + 1], 0.0)
        cells[k, 4:5] = smoothing[k : k + 1]
    fill_outbox(peers, export, cells, outbox)
    greet(regions, peers)
    start_exchange(regions, peers, cells, outbox, table, sems)

    live = active[...] > 0
    row = lax.broadcasted_iota(jnp.int32, (CAP, CAP), 0)
    col = lax.broadcasted_iota(jnp.int32, (CAP, CAP), 1)
    upper = jnp.where(row <= col, 1.0, 0.0)
    ordinal = jnp.dot(jnp.where(live, 1.0, 0.0), upper, preferred_element_type=F32)
    place = jnp.where(live, ordinal - 1.0, -1.0)
    rank[...] = place
    sub = lax.broadcasted_iota(jnp.int32, (8, CAP), 0)
    for k in range(C_DEV):
        groups[k] = (jnp.sum(active[k : k + 1]) + (GROUP - 1)) // GROUP
        fields = jnp.where(sub == 3, energy[k : k + 1], cells[k])
        picked = jnp.where(place[k : k + 1] == row.astype(F32), 1.0, 0.0)
        comp[k] = lax.dot_general(
            picked, fields, (((1,), (1,)), ((), ())),
            precision=lax.Precision.HIGHEST, preferred_element_type=F32,
        )
    finish_exchange(regions, peers, cells, outbox, table, sems)


def moving_kernel(
    regions, peers, export, energy, density, table, cells, outbox, sems
):
    for k in range(C_DEV):
        cells[k, 0:1] = energy[k : k + 1]
        cells[k, 1:2] = density[k : k + 1]
    fill_outbox(peers, export, cells, outbox)
    greet(regions, peers)
    start_exchange(regions, peers, cells, outbox, table, sems)
    finish_exchange(regions, peers, cells, outbox, table, sems)


def fill_shifts(shifts):
    sub = lax.broadcasted_iota(jnp.int32, (8, CAP), 0)
    for s in range(NB):
        offset = (s // 9 - 1, s // 3 % 3 - 1, s % 3 - 1)
        shifts[s] = jnp.where(
            sub == 0, float(offset[0]),
            jnp.where(sub == 1, float(offset[1]), jnp.where(sub == 2, float(offset[2]), 0.0)),
        )


def wide(column):
    return jnp.broadcast_to(column, (GROUP, CAP))


def density_kernel(
    source, shift, groups, table, comp, rank, active, density_old,
    density, comp_density, shifts, near,
):
    fill_shifts(shifts)
    sub = lax.broadcasted_iota(jnp.int32, (GROUP, CAP), 0)
    cube = 4.0 ** (-1.0 / 3.0)

    def cell(k, carry):
        for n in range(NB):
            near[n] = table[source[k, n]] + shifts[shift[k, n]]
        place = rank[pl.ds(k, 1), :]

        def group(g, total):
            at = pl.multiple_of(g * GROUP, GROUP)
            tile = comp[k, pl.ds(at, GROUP), :]
            x, y, z, h = (wide(tile[:, f : f + 1]) for f in (0, 1, 2, 4))
            inverse = 1.0 / h
            scaled = cube * inverse
            partial = jnp.zeros((GROUP, CAP), F32)
            for n in range(NB):
                dx, dy, dz = x - near[n, 0:1], y - near[n, 1:2], z - near[n, 2:3]
                square = jnp.maximum(dx * dx + dy * dy + dz * dz, TINY)
                radius = square * lax.rsqrt(square)
                outer = jnp.maximum(2.0 * cube - radius * scaled, 0.0)
                inner = jnp.maximum(1.0 - radius * inverse, 0.0)
                value = outer * outer * outer - inner * inner * inner
                partial += near[n, 3:4] * value
            norm = inverse * inverse * inverse * (1.0 / math.pi)
            found = jnp.sum(partial, axis=1, keepdims=True) * norm
            comp_density[k, pl.ds(at, GROUP), :] = found
            here = place == (sub + at).astype(F32)
            return total + jnp.where(here, found, 0.0)

        total = lax.fori_loop(0, groups[k], group, jnp.zeros((GROUP, CAP), F32))
        summed = jnp.sum(total, axis=0, keepdims=True)
        mine = pl.ds(k, 1)
        density[mine, :] = jnp.where(active[mine, :] > 0, summed, density_old[mine, :])
        return carry

    lax.fori_loop(0, C_DEV, cell, 0)


def force_kernel(
    source, shift, groups, table, moving, comp, comp_density, rank, velocity, time_bin,
    acceleration, kicked, shifts, derived, near, more,
):
    fill_shifts(shifts)
    sub = lax.broadcasted_iota(jnp.int32, (GROUP, CAP), 0)

    def derive(s, carry):
        h, m = table[s, 4:5], table[s, 3:4]
        e, rho = moving[s, 0:1], moving[s, 1:2]
        inverse = 1.0 / h
        second = inverse * inverse
        derived[s, 0:1] = second
        derived[s, 1:2] = second * inverse
        derived[s, 2:3] = 0.05 * h
        derived[s, 3:4] = m * (1.5 / math.pi)
        derived[s, 4:5] = (ADIABATIC - 1.0) * e / rho
        derived[s, 5:6] = 0.025 * jnp.sqrt(ADIABATIC * (ADIABATIC - 1.0) * e)
        derived[s, 6:7] = rho * (1.0 / 400.0)
        return carry

    lax.fori_loop(0, table.shape[0], derive, 0, unroll=6)

    def cell(k, carry):
        for n in range(NB):
            s = source[k, n]
            near[n] = table[s] + shifts[shift[k, n]]
            more[n] = derived[s]
        place = rank[pl.ds(k, 1), :]

        def group(g, totals):
            at = pl.multiple_of(g * GROUP, GROUP)
            tile = comp[k, pl.ds(at, GROUP), :]
            x, y, z, e, h, vx, vy, vz = (wide(tile[:, f : f + 1]) for f in range(8))
            rho = comp_density[k, pl.ds(at, GROUP), :]
            inverse = 1.0 / h
            second = inverse * inverse
            third = second * inverse
            small = 0.05 * h
            press = (ADIABATIC - 1.0) * e / rho
            sound = 0.025 * jnp.sqrt(ADIABATIC * (ADIABATIC - 1.0) * e)
            thin = rho * (1.0 / 400.0)
            ax = ay = az = jnp.zeros((GROUP, CAP), F32)
            for n in range(NB):
                dx, dy, dz = x - near[n, 0:1], y - near[n, 1:2], z - near[n, 2:3]
                square = jnp.maximum(dx * dx + dy * dy + dz * dz, TINY)
                over = lax.rsqrt(square)
                radius = square * over
                reach = radius * third
                outer = jnp.maximum(second - 0.5 * reach, 0.0)
                inner = jnp.maximum(second - reach, 0.0)
                slope = outer * outer - inner * inner
                second_j = more[n, 0:1]
                reach = radius * more[n, 1:2]
                outer = jnp.maximum(second_j - 0.5 * reach, 0.0)
                inner = jnp.maximum(second_j - reach, 0.0)
                slope += outer * outer - inner * inner
                approach = (
                    (vx - near[n, 5:6]) * dx
                    + (vy - near[n, 6:7]) * dy
                    + (vz - near[n, 7:8]) * dz
                )
                mean = small + more[n, 2:3]
                mu = mean * jnp.minimum(approach, 0.0) * (1.0 / (square + mean * mean))
                viscous = mu * (mu - (sound + more[n, 5:6])) * (1.0 / (thin + more[n, 6:7]))
                weight = more[n, 3:4] * (press + more[n, 4:5] + viscous) * (slope * over)
                ax += weight * dx
                ay += weight * dy
                az += weight * dz
            here = place == (sub + at).astype(F32)
            return tuple(
                total + jnp.where(here, jnp.sum(part, axis=1, keepdims=True), 0.0)
                for total, part in zip(totals, (ax, ay, az))
            )

        none = jnp.zeros((GROUP, CAP), F32)
        totals = lax.fori_loop(0, groups[k], group, (none, none, none))
        mine = pl.ds(k, 1)
        step = STEP_MAX * jnp.exp2(-time_bin[mine, :].astype(F32))
        for i in range(3):
            found = jnp.sum(totals[i], axis=0, keepdims=True)
            acceleration[i, mine, :] = found
            kicked[i, mine, :] = velocity[i, mine, :] + found * step
        return carry

    lax.fori_loop(0, C_DEV, cell, 0)


def shards(
    regions, peers,
    position, velocity, smoothing, particle_mass, energy, density_old, cell_count, active,
    time_bin, pair_source, pair_shift, export,
):
    size = C_DEV + 2 * peers + 2
    vmem = pl.BlockSpec(memory_space=pltpu.VMEM)
    smem = pl.BlockSpec(memory_space=pltpu.SMEM)

    def shape(*dims, dtype=F32):
        return jax.ShapeDtypeStruct(dims, dtype)

    def exchange_scratch(rows):
        return [
            pltpu.VMEM((C_DEV, rows, CAP), F32),
            pltpu.VMEM((peers, 2, rows, CAP), F32),
            pltpu.SemaphoreType.DMA((6,)),
        ]

    limit = 48 << 20
    table, comp, rank, groups = pl.pallas_call(
        functools.partial(static_kernel, regions, peers),
        out_shape=[
            shape(size, 8, CAP), shape(C_DEV, CAP, 8), shape(C_DEV, CAP),
            shape(C_DEV, dtype=jnp.int32),
        ],
        in_specs=[smem, smem] + [vmem] * 6,
        out_specs=[vmem, vmem, vmem, smem],
        scratch_shapes=exchange_scratch(8),
        compiler_params=pltpu.CompilerParams(
            collective_id=0, has_side_effects=True, vmem_limit_bytes=limit
        ),
    )(export, cell_count, position, velocity, smoothing, particle_mass, energy, active)
    density, comp_density = pl.pallas_call(
        density_kernel,
        out_shape=[shape(C_DEV, CAP), shape(C_DEV, CAP, CAP)],
        in_specs=[smem] * 3 + [vmem] * 5,
        out_specs=[vmem, vmem],
        scratch_shapes=[pltpu.VMEM((NB, 8, CAP), F32), pltpu.VMEM((NB, 8, CAP), F32)],
        compiler_params=pltpu.CompilerParams(vmem_limit_bytes=limit),
    )(pair_source, pair_shift, groups, table, comp, rank, active, density_old)
    moving = pl.pallas_call(
        functools.partial(moving_kernel, regions, peers),
        out_shape=shape(size, 2, CAP),
        in_specs=[smem, vmem, vmem],
        out_specs=vmem,
        scratch_shapes=exchange_scratch(2),
        compiler_params=pltpu.CompilerParams(
            collective_id=1, has_side_effects=True, vmem_limit_bytes=limit
        ),
    )(export, energy, density)
    acceleration, kicked = pl.pallas_call(
        force_kernel,
        out_shape=[shape(3, C_DEV, CAP), shape(3, C_DEV, CAP)],
        in_specs=[smem] * 3 + [vmem] * 7,
        out_specs=[vmem, vmem],
        scratch_shapes=[
            pltpu.VMEM((NB, 8, CAP), F32),
            pltpu.VMEM((size, 8, CAP), F32),
            pltpu.VMEM((NB, 8, CAP), F32),
            pltpu.VMEM((NB, 8, CAP), F32),
        ],
        compiler_params=pltpu.CompilerParams(vmem_limit_bytes=limit),
    )(
        pair_source, pair_shift, groups, table, moving, comp, comp_density, rank, velocity,
        time_bin,
    )
    return density, acceleration, kicked


def solution(mesh):
    both = ("region", "cell")
    flat, wide_rows = P(both, None), P(None, both, None)
    return jax.shard_map(
        functools.partial(shards, mesh.shape["region"], mesh.shape["cell"]),
        mesh=mesh,
        in_specs=(
            wide_rows, wide_rows, flat, flat, flat, flat, P(both), flat, flat, flat, flat, flat,
        ),
        out_specs=(flat, wide_rows, wide_rows),
        check_vma=False,
    )
```

time: 169 us -> 73.9 us (0.44)
  the two profiles are of different devices: /device:TPU:57 before, /device:TPU:25 now
where the time goes in v1:
time: 73.9 us; the launch traced here: 73.5 us
  Pallas kernels  69.2 us (94%)
  local copies, waits for them, and re-layouts  3.55 us (5%)
  between operations  0.76 us (1%)
    pallas_call x1, Pallas kernels, shards(): pl.pallas_call(functools.partial(static_kernel, regions, peers), out_shap...  28.5 us
    pallas_call x1, Pallas kernels, shards(): pl.pallas_call(force_kernel, out_shape=[shape(3, C_DEV, CAP), shape(3, C_...  16.4 us
    pallas_call x1, Pallas kernels, shards(): pl.pallas_call(functools.partial(moving_kernel, regions, peers), out_shap...  13.9 us
    pallas_call x1, Pallas kernels, shards(): pl.pallas_call(density_kernel, out_shape=[shape(C_DEV, CAP), shape(C_DEV,...  10.4 us
    unnamed x25, local copies, waits for them, and re-layouts  3.55 us

profile of v1, /device:TPU:25, one launch (start us, length us, event | category | flops | bytes accessed | tf_op | source)
XLA Modules:
  0.0 73.5 jit_solution(4107094219863009576)
XLA Ops:
  0.6 0.0 copy-start.3
  0.6 0.0 copy-start.4
  0.7 0.0 copy-start
  0.7 0.0 copy-start.11
  0.7 0.0 copy-start.5
  0.7 0.8 %copy.15.export = s32[64,2]{1,0:T(8,128)S(1)} copy(s32[64,2]{0,1:T(2,128)} %param.23) | data formatting | bytes 1024 | tf_op args[11]
  1.5 0.0 copy-done.3
  1.5 0.0 copy-done.4
  1.5 0.0 copy-done
  1.5 0.0 copy-done.11
  1.5 0.0 copy-done.5
  1.5 0.0 copy-start.8
  1.5 0.7 copy-done.8
  2.2 0.7 copy-done.9
  2.9 28.5 %shard_map.139 = (f32[138,8,128]{2,1,0:T(8,128)S(1)}, f32[8,128,8]{2,1,0:T(8,128)S(1)}, f32[8,128]{1,0:T(8,128)S(1)}, s32[8]{0:T(128)S(1)}) custom-call(s32[64,2]{1,0:T(8,128)S(1)} %copy.15.export, s32[8]{0:T(128)S(1)} %copy-done.11, f32[3,8,128]{2,1,0:T(8,128)S(1)} %copy-done.5, f32[3,8,128]{2,1,0:T(8,128)S(1)} %copy-done, f32[8,128]{1,0:T(8,128)S(1)} %copy-done.8, ...), custom_call_target="tpu_custom_call" | custom-call | tf_op jit(solution)/shard_map/pallas_call | solution.py:317
  31.4 0.0 copy-start.1
  31.4 0.0 copy-done.2
  31.5 0.0 copy-done.6
  31.5 0.7 copy-done.1
  32.1 10.4 %shard_map.140 = (f32[8,128]{1,0:T(8,128)}, f32[8,128,128]{2,1,0:T(8,128)S(1)}) custom-call(s32[8,27]{1,0:T(8,128)S(1)} %copy-done.1, s32[8,27]{1,0:T(8,128)S(1)} %copy-done.2, s32[8]{0:T(128)S(1)} %get-tuple-element.11.groups, f32[138,8,128]{2,1,0:T(8,128)S(1)} %get-tuple-element.12.table, f32[8,128,8]{2,1,0:T(8,128)S(1)} %get-tuple-element.13.comp, ...), custom_call_target="tpu_custom_call" | custom-call | tf_op jit(solution)/shard_map/pallas_call | solution.py:330
  42.6 0.7 copy-done.10
  43.2 13.9 %shard_map.141.moving = f32[138,2,128]{2,1,0:T(2,128)S(1)} custom-call(s32[64,2]{1,0:T(8,128)S(1)} %copy.15.export, f32[8,128]{1,0:T(8,128)S(1)} %copy-done.4, f32[8,128]{1,0:T(8,128)S(1)} %copy-done.10), custom_call_target="tpu_custom_call" | custom-call | tf_op jit(solution)/shard_map/pallas_call | solution.py:338
  57.2 0.0 copy-done.7
  57.2 16.4 %shard_map.142 = (f32[3,8,128]{2,1,0:T(8,128)}, f32[3,8,128]{2,1,0:T(8,128)}) custom-call(s32[8,27]{1,0:T(8,128)S(1)} %copy-done.1, s32[8,27]{1,0:T(8,128)S(1)} %copy-done.2, s32[8]{0:T(128)S(1)} %get-tuple-element.11.groups, f32[138,8,128]{2,1,0:T(8,128)S(1)} %get-tuple-element.12.table, f32[138,2,128]{2,1,0:T(2,128)S(1)} %shard_map.141.moving, ...), custom_call_target="tpu_custom_call" | custom-call | tf_op jit(solution)/shard_map/pallas_call | solution.py:348
  (5 shorter events, 0.0 us)
Async XLA Ops:
  0.6 0.8 %copy-start.3 = (s32[8,128]{1,0:T(8,128)S(1)}, s32[8,128]{1,0:T(8,128)}, u32[]{:S(2)}) copy-start(s32[8,128]{1,0:T(8,128)} %active.3) | copy-start | bytes 12292
  0.6 0.8 %copy-start.4 = (f32[8,128]{1,0:T(8,128)S(1)}, f32[8,128]{1,0:T(8,128)}, u32[]{:S(2)}) copy-start(f32[8,128]{1,0:T(8,128)} %energy.3) | copy-start | bytes 12292
  0.7 0.8 %copy-start = (f32[3,8,128]{2,1,0:T(8,128)S(1)}, f32[3,8,128]{2,1,0:T(8,128)}, u32[]{:S(2)}) copy-start(f32[3,8,128]{2,1,0:T(8,128)} %velocity.3) | copy-start | bytes 36868
  0.7 0.8 %copy-start.11 = (s32[8]{0:T(128)S(1)}, s32[8]{0:T(128)}, u32[]{:S(2)}) copy-start(s32[8]{0:T(128)} %count.1) | copy-start | bytes 100
  0.7 0.8 %copy-start.5 = (f32[3,8,128]{2,1,0:T(8,128)S(1)}, f32[3,8,128]{2,1,0:T(8,128)}, u32[]{:S(2)}) copy-start(f32[3,8,128]{2,1,0:T(8,128)} %position.1) | copy-start | bytes 36868
  1.5 0.7 copy-start.8
  2.2 0.7 copy-start.9
  2.9 28.6 %copy-start.2 = (s32[8,27]{1,0:T(8,128)S(1)}, s32[8,27]{1,0:T(8,128)}, u32[]{:S(2)}) copy-start(s32[8,27]{1,0:T(8,128)} %shift.3) | copy-start | bytes 2596
  2.9 28.6 %copy-start.6 = (f32[8,128]{1,0:T(8,128)S(1)}, f32[8,128]{1,0:T(8,128)}, u32[]{:S(2)}) copy-start(f32[8,128]{1,0:T(8,128)} %density_old.1) | copy-start | bytes 12292
  31.4 0.7 copy-start.1
  42.6 0.7 copy-start.10
  43.2 13.9 %copy-start.7 = (s32[8,128]{1,0:T(8,128)S(1)}, s32[8,128]{1,0:T(8,128)}, u32[]{:S(2)}) copy-start(s32[8,128]{1,0:T(8,128)} %time_bin.1) | copy-start | bytes 12292

commit v2 on v1

v2 whole, which is shorter than its diff:
```python
import functools
import math

import jax
import jax.numpy as jnp
from jax import lax
from jax.experimental import pallas as pl
from jax.experimental.pallas import tpu as pltpu
from jax.sharding import PartitionSpec as P

MESH = pl.DeviceIdType.MESH
C_DEV = 8
CAP = 128
NB = 27
GROUP = 8
PLANE = 8
ORDER = (1, 7, 2, 6, 3, 5, 4)
BATCH = 4
ADIABATIC = 5.0 / 3.0
STEP_MAX = 0.2
TINY = 1e-30
F32 = jnp.float32
SHIFT_AT, GROUP_AT = 32, 64


def place():
    r, c = lax.axis_index("region"), lax.axis_index("cell")
    return r, lax.div(c, PLANE), lax.rem(c, PLANE)


def along(z, u, planes, ahead):
    return lax.rem(z + ahead, planes) * PLANE + u


def across(z, u, ahead):
    return z * PLANE + lax.rem(u + ahead, PLANE)


def greet(regions, planes):
    r, z, u = place()
    barrier = pltpu.get_barrier_semaphore()
    for ahead in range(1, planes):
        pl.semaphore_signal(
            barrier, inc=1, device_id=(r, along(z, u, planes, ahead)), device_id_type=MESH
        )
    for ahead in range(1, PLANE):
        pl.semaphore_signal(
            barrier, inc=1, device_id=(r, across(z, u, ahead)), device_id_type=MESH
        )
    for ahead in (1, regions - 1):
        pl.semaphore_signal(
            barrier, inc=1, device_id=(lax.rem(r + ahead, regions), z * PLANE + u),
            device_id_type=MESH,
        )
    return lambda: pl.semaphore_wait(barrier, planes + PLANE)


def region_copies(regions, cells, table, sems):
    r, z, u = place()
    size = table.shape[0]
    up = pltpu.make_async_remote_copy(
        src_ref=cells.at[pl.ds(C_DEV - 1, 1)],
        dst_ref=table.at[pl.ds(size - 2, 1)],
        send_sem=sems.at[0],
        recv_sem=sems.at[1],
        device_id=(lax.rem(r + 1, regions), z * PLANE + u),
        device_id_type=MESH,
    )
    down = pltpu.make_async_remote_copy(
        src_ref=cells.at[pl.ds(0, 1)],
        dst_ref=table.at[pl.ds(size - 1, 1)],
        send_sem=sems.at[2],
        recv_sem=sems.at[3],
        device_id=(lax.rem(r + regions - 1, regions), z * PLANE + u),
        device_id_type=MESH,
    )
    return up, down


def send_along(planes, ahead, source, target, send_sem, recv_sem):
    r, z, u = place()
    return pltpu.make_async_remote_copy(
        src_ref=source, dst_ref=target, send_sem=send_sem, recv_sem=recv_sem,
        device_id=(r, along(z, u, planes, ahead)), device_id_type=MESH,
    )


def send_across(first, cells, outbox, table, send_sem, recv_sem):
    r, z, u = place()
    rows = 2 * BATCH

    def send(ahead, carry):
        to = lax.rem(u + ahead, PLANE)
        pltpu.make_async_remote_copy(
            src_ref=outbox.at[to, pl.ds(2 * first, rows)],
            dst_ref=table.at[pl.ds(C_DEV + 2 * cells * u + 2 * first, rows)],
            send_sem=send_sem, recv_sem=recv_sem,
            device_id=(r, z * PLANE + to), device_id_type=MESH,
        ).start()
        return carry

    lax.fori_loop(1, PLANE, send, 0)


def choose(slot, export, cells, outbox):
    r, z, u = place()

    def fill(to, carry):
        for q in range(2):
            outbox[to, 2 * slot + q] = cells[export[slot, q, z * PLANE + to]]
        return carry

    lax.fori_loop(0, PLANE, fill, 0, unroll=True)


def keep_own(planes, cells, outbox, table):
    r, z, u = place()
    for k in range(C_DEV):
        table[k] = cells[k]
    for i in range(2 * planes):
        table[C_DEV + 2 * planes * u + i] = outbox[u, i]


def drain(planes, outbox, table, send_sem, recv_sem):
    sent = outbox.at[pl.ds(0, PLANE - 1)]
    pltpu.make_async_copy(sent, sent, send_sem).wait()
    landed = table.at[pl.ds(0, 2 * planes * (PLANE - 1))]
    pltpu.make_async_copy(landed, landed, recv_sem).wait()


def static_kernel(
    regions, planes,
    position, velocity, smoothing, mass, energy, active, count, export, source, shift, old,
    table, comp, rank, plan, exports, energy_v, old_v,
    position_v, velocity_v, smoothing_v, mass_v, active_v, count_s, source_v, shift_v,
    cells, exports_s, outbox, *rest,
):
    land, (fetch_sems, region_sems, export_sems, along_send, along_recv, across_sems, own_sem) = (
        rest[: planes - 1], rest[planes - 1 :]
    )
    wait_for_all = greet(regions, planes)
    fetches = [
        pltpu.make_async_copy(a, b, fetch_sems.at[i])
        for i, (a, b) in enumerate((
            (position, position_v), (smoothing, smoothing_v), (mass, mass_v), (count, count_s),
            (velocity, velocity_v), (export, exports.at[0]), (energy, energy_v),
            (active, active_v), (source, source_v), (shift, shift_v), (old, old_v),
        ))
    ]
    for fetch in fetches:
        fetch.start()
    for fetch in fetches:
        fetch.wait()
    slot = lax.broadcasted_iota(jnp.int32, (1, CAP), 1)
    for k in range(C_DEV):
        for i in range(3):
            cells[k, i : i + 1] = position_v[i, k : k + 1]
            cells[k, 5 + i : 6 + i] = velocity_v[i, k : k + 1]
        cells[k, 3:4] = jnp.where(slot < count_s[k], mass_v[k : k + 1], 0.0)
        cells[k, 4:5] = smoothing_v[k : k + 1]
    wait_for_all()
    regionals = region_copies(regions, cells, table, region_sems)
    lists = [
        send_along(
            planes, ahead, exports.at[0], exports.at[i + 1], export_sems.at[0], export_sems.at[1]
        )
        for i, ahead in enumerate(ORDER)
    ]
    blocks = [
        send_along(planes, ahead, cells, land[i], along_send.at[i], along_recv.at[i])
        for i, ahead in enumerate(ORDER)
    ]
    for copy in lists + blocks[:2] + list(regionals) + blocks[2:]:
        copy.start()

    live = active_v[...] > 0
    row = lax.broadcasted_iota(jnp.int32, (CAP, CAP), 0)
    col = lax.broadcasted_iota(jnp.int32, (CAP, CAP), 1)
    upper = jnp.where(row <= col, 1.0, 0.0)
    ordinal = jnp.dot(jnp.where(live, 1.0, 0.0), upper, preferred_element_type=F32)
    where_to = jnp.where(live, ordinal - 1.0, -1000.0)
    rank[...] = where_to
    groups = (jnp.sum(active_v[...], axis=1, keepdims=True) + (GROUP - 1)) // GROUP
    r, z, u = place()
    named = source_v[...]
    other = named - C_DEV
    behind = jnp.bitwise_and(z + planes - jnp.right_shift(other, 4), planes - 1)
    slot_of = jnp.zeros_like(behind)
    for i, ahead in enumerate(ORDER):
        slot_of = jnp.where(behind == ahead, i + 1, slot_of)
    peer = jnp.bitwise_and(jnp.right_shift(other, 1), PLANE - 1)
    moved = C_DEV + 2 * planes * peer + 2 * slot_of + jnp.bitwise_and(other, 1)
    inside = jnp.logical_and(named >= C_DEV, named < C_DEV + 2 * planes * PLANE)
    plan[:, 0:NB] = jnp.where(inside, moved, named)
    plan[:, SHIFT_AT : SHIFT_AT + NB] = shift_v[...]
    plan[:, GROUP_AT : GROUP_AT + 1] = groups

    drained = exports.at[pl.ds(1, planes - 1)]
    pltpu.make_async_copy(drained, drained, export_sems.at[1]).wait()
    pltpu.make_async_copy(drained, drained, export_sems.at[0]).wait()
    to_scalar = pltpu.make_async_copy(exports, exports_s, own_sem)
    to_scalar.start()
    to_scalar.wait()
    choose(0, exports_s, cells, outbox)
    sub = lax.broadcasted_iota(jnp.int32, (8, CAP), 0)

    def compact(k):
        fields = jnp.where(sub == 3, energy_v[k : k + 1], cells[k])
        picked = jnp.where(where_to[k : k + 1] == row.astype(F32), 1.0, 0.0)
        comp[k] = lax.dot_general(
            picked, fields, (((1,), (1,)), ((), ())),
            precision=lax.Precision.HIGHEST, preferred_element_type=F32,
        )

    for i in range(planes - 1):
        compact(i)
        blocks[i].wait_recv()
        choose(i + 1, exports_s, land[i], outbox)
        if (i + 2) % BATCH == 0:
            send_across(
                i + 2 - BATCH, planes, outbox, table, across_sems.at[0], across_sems.at[1]
            )
    compact(planes - 1)
    keep_own(planes, cells, outbox, table)
    for copy in regionals:
        copy.wait()
    for copy in blocks:
        copy.wait_send()
    drain(planes, outbox, table, across_sems.at[0], across_sems.at[1])


def moving_kernel(
    regions, planes, exports, energy, density, table,
    cells, land, outbox, region_sems, along_sems, across_sems,
):
    wait_for_all = greet(regions, planes)
    for k in range(C_DEV):
        cells[k, 0:1] = energy[k : k + 1]
        cells[k, 1:2] = density[k : k + 1]
    wait_for_all()
    regionals = region_copies(regions, cells, table, region_sems)
    blocks = [
        send_along(planes, ahead, cells, land.at[i], along_sems.at[0], along_sems.at[1])
        for i, ahead in enumerate(ORDER)
    ]
    for copy in blocks + list(regionals):
        copy.start()
    choose(0, exports, cells, outbox)
    pltpu.make_async_copy(land, land, along_sems.at[1]).wait()
    for i in range(planes - 1):
        choose(i + 1, exports, land.at[i], outbox)
        if (i + 2) % BATCH == 0:
            send_across(
                i + 2 - BATCH, planes, outbox, table, across_sems.at[0], across_sems.at[1]
            )
    keep_own(planes, cells, outbox, table)
    for copy in regionals:
        copy.wait()
    pltpu.make_async_copy(land, land, along_sems.at[0]).wait()
    drain(planes, outbox, table, across_sems.at[0], across_sems.at[1])


def fill_shifts(shifts):
    sub = lax.broadcasted_iota(jnp.int32, (8, CAP), 0)
    for s in range(NB):
        offset = (s // 9 - 1, s // 3 % 3 - 1, s % 3 - 1)
        shifts[s] = jnp.where(
            sub == 0, float(offset[0]),
            jnp.where(sub == 1, float(offset[1]), jnp.where(sub == 2, float(offset[2]), 0.0)),
        )


def wide(column):
    return jnp.broadcast_to(column, (GROUP, CAP))


def gather(plan, k, block_of, near):
    for n in range(NB):
        near[n] = block_of(plan[k, n], n)


def density_kernel(
    plan, table, comp, rank, density_old,
    density, density_too, comp_density,
    shifts, near, total,
):
    fill_shifts(shifts)
    sub = lax.broadcasted_iota(jnp.int32, (GROUP, CAP), 0)
    cube = 4.0 ** (-1.0 / 3.0)

    def cell(k, carry):
        gather(plan, k, lambda s, n: table[s] + shifts[plan[k, SHIFT_AT + n]], near)
        ranks = rank[pl.ds(k, 1), :]
        total[...] = jnp.zeros((GROUP, CAP), F32)
        groups = plan[k, GROUP_AT]

        def setup(g):
            at = pl.multiple_of(jnp.minimum(g, CAP // GROUP - 1) * GROUP, GROUP)
            tile = comp[k, pl.ds(at, GROUP), :]
            x, y, z, h = (wide(tile[:, f : f + 1]) for f in (0, 1, 2, 4))
            return x, y, z, 1.0 / h

        def finish(g, partial, norm):
            found = jnp.sum(partial, axis=1, keepdims=True) * norm
            at = pl.multiple_of(jnp.maximum(g, 0) * GROUP, GROUP)
            comp_density[k, pl.ds(at, GROUP), :] = found
            here = ranks == (sub + g * GROUP).astype(F32)
            total[...] += jnp.where(here, found, 0.0)

        def run(size):
            def group(g, carry):
                (x, y, z, inverse), partial, norm = carry
                finish(g - 1, partial, norm)
                following = setup(g + 1)
                scaled = cube * inverse
                partial = jnp.zeros((GROUP, CAP), F32)
                for n in range(size):
                    dx, dy, dz = x - near[n, 0:1], y - near[n, 1:2], z - near[n, 2:3]
                    square = jnp.maximum(dx * dx + dy * dy + dz * dz, TINY)
                    radius = square * lax.rsqrt(square)
                    outer = jnp.maximum(2.0 * cube - radius * scaled, 0.0)
                    inner = jnp.maximum(1.0 - radius * inverse, 0.0)
                    value = outer * outer * outer - inner * inner * inner
                    partial += near[n, 3:4] * value
                return following, partial, inverse * inverse * inverse * (1.0 / math.pi)

            none = jnp.zeros((GROUP, CAP), F32)
            _, partial, norm = lax.fori_loop(0, groups, group, (setup(0), none, none))
            finish(groups - 1, partial, norm)

        run(NB)
        summed = jnp.sum(total[...], axis=0, keepdims=True)
        mine = pl.ds(k, 1)
        found = jnp.where(ranks >= 0.0, summed, density_old[mine, :])
        density[mine, :] = found
        density_too[mine, :] = found
        return carry

    lax.fori_loop(0, C_DEV, cell, 0)


def force_kernel(
    plan, table, moving, comp, comp_density, rank, velocity, time_bin,
    acceleration, kicked, shifts, near, derived, more, total,
):
    sub = lax.broadcasted_iota(jnp.int32, (GROUP, CAP), 0)

    def derive(s, carry):
        h, m = table[s, 4:5], table[s, 3:4]
        e, rho = moving[s, 0:1], moving[s, 1:2]
        inverse = 1.0 / h
        second = inverse * inverse
        derived[s, 0:1] = second
        derived[s, 1:2] = second * inverse
        derived[s, 2:3] = 0.05 * h
        derived[s, 3:4] = m * (1.5 / math.pi)
        derived[s, 4:5] = (ADIABATIC - 1.0) * e / rho
        derived[s, 5:6] = 0.025 * jnp.sqrt(ADIABATIC * (ADIABATIC - 1.0) * e)
        derived[s, 6:7] = rho * (1.0 / 400.0)
        derived[s, 7:8] = rho
        return carry

    fill_shifts(shifts)
    lax.fori_loop(0, table.shape[0], derive, 0, unroll=6)

    def cell(k, carry):
        gather(plan, k, lambda s, n: table[s] + shifts[plan[k, SHIFT_AT + n]], near)
        gather(plan, k, lambda s, n: derived[s], more)
        ranks = rank[pl.ds(k, 1), :]
        total[...] = jnp.zeros((3, GROUP, CAP), F32)
        groups = plan[k, GROUP_AT]

        def setup(g):
            at = pl.multiple_of(jnp.minimum(g, CAP // GROUP - 1) * GROUP, GROUP)
            tile = comp[k, pl.ds(at, GROUP), :]
            x, y, z, e, h, vx, vy, vz = (wide(tile[:, f : f + 1]) for f in range(8))
            rho = comp_density[k, pl.ds(at, GROUP), :]
            inverse = 1.0 / h
            second = inverse * inverse
            press = (ADIABATIC - 1.0) * e / rho
            sound = 0.025 * jnp.sqrt(ADIABATIC * (ADIABATIC - 1.0) * e)
            return (
                x, y, z, vx, vy, vz, second, second * inverse, 0.05 * h, press, sound,
                rho * (1.0 / 400.0),
            )

        def finish(g, parts):
            here = ranks == (sub + g * GROUP).astype(F32)
            for i in range(3):
                total[i] += jnp.where(here, jnp.sum(parts[i], axis=1, keepdims=True), 0.0)

        def run(size):
            def group(g, carry):
                (x, y, z, vx, vy, vz, second, third, small, press, sound, thin), parts = carry
                finish(g - 1, parts)
                following = setup(g + 1)
                ax = ay = az = jnp.zeros((GROUP, CAP), F32)
                for n in range(size):
                    dx, dy, dz = x - near[n, 0:1], y - near[n, 1:2], z - near[n, 2:3]
                    square = jnp.maximum(dx * dx + dy * dy + dz * dz, TINY)
                    over = lax.rsqrt(square)
                    radius = square * over
                    reach = radius * third
                    outer = jnp.maximum(second - 0.5 * reach, 0.0)
                    inner = jnp.maximum(second - reach, 0.0)
                    slope = outer * outer - inner * inner
                    second_j = more[n, 0:1]
                    reach = radius * more[n, 1:2]
                    outer = jnp.maximum(second_j - 0.5 * reach, 0.0)
                    inner = jnp.maximum(second_j - reach, 0.0)
                    slope += outer * outer - inner * inner
                    approach = (
                        (vx - near[n, 5:6]) * dx
                        + (vy - near[n, 6:7]) * dy
                        + (vz - near[n, 7:8]) * dz
                    )
                    mean = small + more[n, 2:3]
                    mu = mean * jnp.minimum(approach, 0.0) * (1.0 / (square + mean * mean))
                    viscous = mu * (mu - (sound + more[n, 5:6])) * (1.0 / (thin + more[n, 6:7]))
                    weight = more[n, 3:4] * (press + more[n, 4:5] + viscous) * (slope * over)
                    ax += weight * dx
                    ay += weight * dy
                    az += weight * dz
                return following, (ax, ay, az)

            none = jnp.zeros((GROUP, CAP), F32)
            _, parts = lax.fori_loop(0, groups, group, (setup(0), (none, none, none)))
            finish(groups - 1, parts)

        run(NB)
        mine = pl.ds(k, 1)
        step = STEP_MAX * jnp.exp2(-time_bin[mine, :].astype(F32))
        for i in range(3):
            found = jnp.sum(total[i], axis=0, keepdims=True)
            acceleration[i, mine, :] = found
            kicked[i, mine, :] = velocity[i, mine, :] + found * step
        return carry

    lax.fori_loop(0, C_DEV, cell, 0)


def shards(
    regions, planes,
    position, velocity, smoothing, particle_mass, energy, density_old, cell_count, active,
    time_bin, pair_source, pair_shift, export,
):
    size = C_DEV + 2 * planes * PLANE + 2
    vmem = pl.BlockSpec(memory_space=pltpu.VMEM)
    smem = pl.BlockSpec(memory_space=pltpu.SMEM)
    hbm = pl.BlockSpec(memory_space=pltpu.HBM)
    dma = pltpu.SemaphoreType.DMA

    def shape(*dims, dtype=F32):
        return jax.ShapeDtypeStruct(dims, dtype)

    def ints(*dims):
        return pltpu.VMEM(dims, jnp.int32)

    def floats(*dims):
        return pltpu.VMEM(dims, F32)

    limit = 48 << 20
    table, comp, rank, plan, exports, energy, density_old = pl.pallas_call(
        functools.partial(static_kernel, regions, planes),
        out_shape=[
            shape(size, 8, CAP), shape(C_DEV, CAP, 8), shape(C_DEV, CAP),
            shape(C_DEV, CAP, dtype=jnp.int32),
            shape(planes, 2, planes * PLANE, dtype=jnp.int32), shape(C_DEV, CAP), shape(C_DEV, CAP),
        ],
        in_specs=[hbm] * 11,
        out_specs=[vmem] * 7,
        scratch_shapes=[
            floats(3, C_DEV, CAP), floats(3, C_DEV, CAP), floats(C_DEV, CAP), floats(C_DEV, CAP),
            ints(C_DEV, CAP), pltpu.SMEM((C_DEV,), jnp.int32),
            ints(C_DEV, NB), ints(C_DEV, NB),
            floats(C_DEV, 8, CAP), pltpu.SMEM((planes, 2, planes * PLANE), jnp.int32),
            floats(PLANE, 2 * planes, 8, CAP),
            *[floats(C_DEV, 8, CAP) for _ in range(planes - 1)],
            dma((11,)), dma((4,)), dma((2,)), dma((planes - 1,)), dma((planes - 1,)), dma((2,)),
            dma,
        ],
        compiler_params=pltpu.CompilerParams(
            collective_id=0, has_side_effects=True, vmem_limit_bytes=limit
        ),
    )(
        *(
            pltpu.with_memory_space_constraint(x, pltpu.HBM)
            for x in (
                position, velocity, smoothing, particle_mass, energy, active, cell_count, export.T,
                pair_source, pair_shift, density_old,
            )
        )
    )
    density, density_too, comp_density = pl.pallas_call(
        density_kernel,
        out_shape=[shape(C_DEV, CAP), shape(C_DEV, CAP), shape(C_DEV, CAP, CAP)],
        in_specs=[smem] + [vmem] * 4,
        out_specs=[vmem] * 3,
        scratch_shapes=[floats(NB, 8, CAP), floats(NB, 8, CAP), floats(GROUP, CAP)],
        compiler_params=pltpu.CompilerParams(vmem_limit_bytes=limit),
    )(plan, table, comp, rank, density_old)
    moving = pl.pallas_call(
        functools.partial(moving_kernel, regions, planes),
        out_shape=shape(size, 2, CAP),
        in_specs=[smem, vmem, vmem],
        out_specs=vmem,
        scratch_shapes=[
            floats(C_DEV, 2, CAP), floats(planes - 1, C_DEV, 2, CAP),
            floats(PLANE, 2 * planes, 2, CAP), dma((4,)), dma((2,)), dma((2,)),
        ],
        compiler_params=pltpu.CompilerParams(
            collective_id=1, has_side_effects=True, vmem_limit_bytes=limit
        ),
    )(exports, energy, density_too)
    acceleration, kicked = pl.pallas_call(
        force_kernel,
        out_shape=[shape(3, C_DEV, CAP), shape(3, C_DEV, CAP)],
        in_specs=[smem] + [vmem] * 7,
        out_specs=[vmem, vmem],
        scratch_shapes=[
            floats(NB, 8, CAP), floats(NB, 8, CAP), floats(size, 8, CAP), floats(NB, 8, CAP),
            floats(3, GROUP, CAP),
        ],
        compiler_params=pltpu.CompilerParams(vmem_limit_bytes=limit),
    )(plan, table, moving, comp, comp_density, rank, velocity, time_bin)
    return density, acceleration, kicked


def solution(mesh):
    both = ("region", "cell")
    flat, wide_rows = P(both, None), P(None, both, None)
    return jax.shard_map(
        functools.partial(shards, mesh.shape["region"], mesh.shape["cell"] // PLANE),
        mesh=mesh,
        in_specs=(
            wide_rows, wide_rows, flat, flat, flat, flat, P(both), flat, flat, flat, flat, flat,
        ),
        out_specs=(flat, wide_rows, wide_rows),
        check_vma=False,
    )
```

time: 73.9 us -> 56.3 us (0.76)
  the two profiles are of different devices: /device:TPU:25 before, /device:TPU:49 now
where the time goes in v2:
time: 56.3 us; the launch traced here: 56 us
  Pallas kernels  55.4 us (98%)
  between operations  0.67 us (1%)
    pallas_call x1, Pallas kernels, shards(): pl.pallas_call(functools.partial(static_kernel, regions, planes), out_sha...  25.2 us
    pallas_call x1, Pallas kernels, shards(): pl.pallas_call(functools.partial(moving_kernel, regions, planes), out_sha...  14.7 us
    pallas_call x1, Pallas kernels, shards(): pl.pallas_call(force_kernel, out_shape=[shape(3, C_DEV, CAP), shape(3, C_...  10.1 us
    pallas_call x1, Pallas kernels, shards(): pl.pallas_call(density_kernel, out_shape=[shape(C_DEV, CAP), shape(C_DEV,...  5.37 us

profile of v2, /device:TPU:49, one launch (start us, length us, event | category | flops | bytes accessed | tf_op | source)
XLA Modules:
  0.0 56.0 jit_solution(6888667763169547539)
XLA Ops:
  0.6 25.2 %shard_map.139 = (f32[138,8,128]{2,1,0:T(8,128)S(1)}, f32[8,128,8]{2,1,0:T(8,128)S(1)}, f32[8,128]{1,0:T(8,128)S(1)}, s32[8,128]{1,0:T(8,128)S(1)}, s32[8,2,64]{...) custom-call(f32[3,8,128]{2,1,0:T(8,128)} %position.1, f32[3,8,128]{2,1,0:T(8,128)} %velocity.3, ...), custom_call_target="tpu_custom_call" | custom-call | tf_op jit(solution)/shard_map/pallas_call | solution.py:463
  25.8 5.4 %shard_map.140 = (f32[8,128]{1,0:T(8,128)}, f32[8,128]{1,0:T(8,128)S(1)}, f32[8,128,128]{2,1,0:T(8,128)S(1)}) custom-call(s32[8,128]{1,0:T(8,128)S(1)} %get-tuple-element.15.plan, f32[138,8,128]{2,1,0:T(8,128)S(1)} %get-tuple-element.16.table, f32[8,128,8]{2,1,0:T(8,128)S(1)} %get-tuple-element.17.comp, f32[8,128]{1,0:T(8,128)S(1)} %get-tuple-element.18.rank, ...), custom_call_target="tpu_custom_call" | custom-call | tf_op jit(solution)/shard_map/pallas_call | solution.py:494
  31.2 0.0 copy-start
  31.2 0.0 copy-start.1
  31.2 14.7 %shard_map.141.moving = f32[138,2,128]{2,1,0:T(2,128)S(1)} custom-call(s32[8,2,64]{2,1,0:T(2,128)S(1)} %get-tuple-element.21.exports, f32[8,128]{1,0:T(8,128)S(1)} %get-tuple-element.22.energy, f32[8,128]{1,0:T(8,128)S(1)} %get-tuple-element.23.density), custom_call_target="tpu_custom_call" | custom-call | tf_op jit(solution)/shard_map/pallas_call | solution.py:502
  45.9 0.0 copy-done
  45.9 0.0 copy-done.1
  45.9 10.1 %shard_map.142 = (f32[3,8,128]{2,1,0:T(8,128)}, f32[3,8,128]{2,1,0:T(8,128)}) custom-call(s32[8,128]{1,0:T(8,128)S(1)} %get-tuple-element.15.plan, f32[138,8,128]{2,1,0:T(8,128)S(1)} %get-tuple-element.16.table, f32[138,2,128]{2,1,0:T(2,128)S(1)} %shard_map.141.moving, f32[8,128,8]{2,1,0:T(8,128)S(1)} %get-tuple-element.17.comp, ...), custom_call_target="tpu_custom_call" | custom-call | tf_op jit(solution)/shard_map/pallas_call | solution.py:515
Async XLA Ops:
  31.2 14.7 %copy-start = (f32[3,8,128]{2,1,0:T(8,128)S(1)}, f32[3,8,128]{2,1,0:T(8,128)}, u32[]{:S(2)}) copy-start(f32[3,8,128]{2,1,0:T(8,128)} %velocity.3) | copy-start | bytes 36868
  31.2 14.7 %copy-start.1 = (s32[8,128]{1,0:T(8,128)S(1)}, s32[8,128]{1,0:T(8,128)}, u32[]{:S(2)}) copy-start(s32[8,128]{1,0:T(8,128)} %time_bin.1) | copy-start | bytes 12292

commit v3 on v2

--- a/solution.py
+++ b/solution.py
@@ -14,13 +14,19 @@
 NB = 27
 GROUP = 8
 PLANE = 8
-ORDER = (1, 7, 2, 6, 3, 5, 4)
-BATCH = 4
+ORDER = (1, 7, 4, 2, 6, 3, 5)
+BATCH = 2
 ADIABATIC = 5.0 / 3.0
 STEP_MAX = 0.2
 TINY = 1e-30
 F32 = jnp.float32
 SHIFT_AT, GROUP_AT = 32, 64
+SIZES = (8, 12, 15, 16, 17, 18, 19, 20, 22, 24, 27)
+ROWS = NB + 8
+X, Y, Z, INVERSE, VX, VY, VZ, SECOND, THIRD, SMALL, SOUND, HEAT = range(12)
+TARGET = 12
+SOUND_UNIT = 0.025
+DENSITY_UNIT = 1.0 / 400.0
 
 
 def place():
@@ -131,7 +137,7 @@
 def static_kernel(
     regions, planes,
     position, velocity, smoothing, mass, energy, active, count, export, source, shift, old,
-    table, comp, rank, plan, exports, energy_v, old_v,
+    table, targets, rank, plan, exports, energy_v, old_v,
     position_v, velocity_v, smoothing_v, mass_v, active_v, count_s, source_v, shift_v,
     cells, exports_s, outbox, *rest,
 ):
@@ -207,10 +213,22 @@
     def compact(k):
         fields = jnp.where(sub == 3, energy_v[k : k + 1], cells[k])
         picked = jnp.where(where_to[k : k + 1] == row.astype(F32), 1.0, 0.0)
-        comp[k] = lax.dot_general(
+        found = lax.dot_general(
             picked, fields, (((1,), (1,)), ((), ())),
             precision=lax.Precision.HIGHEST, preferred_element_type=F32,
         )
+        x, y, z, e, h, vx, vy, vz = (
+            jnp.broadcast_to(found[:, f : f + 1], (CAP, CAP)) for f in range(8)
+        )
+        inverse = 1.0 / h
+        second = inverse * inverse
+        for at, value in (
+            (X, x), (Y, y), (Z, z), (INVERSE, inverse), (VX, vx), (VY, vy), (VZ, vz),
+            (SECOND, second), (THIRD, second * inverse), (SMALL, 0.05 * h),
+            (SOUND, SOUND_UNIT * jnp.sqrt(ADIABATIC * (ADIABATIC - 1.0) * e)),
+            (HEAT, (ADIABATIC - 1.0) * e),
+        ):
+            targets[at, k] = value
 
     for i in range(planes - 1):
         compact(i)
@@ -229,14 +247,42 @@
     drain(planes, outbox, table, across_sems.at[0], across_sems.at[1])
 
 
+def offsets_of(table, plan):
+    size = table.shape[0]
+    ones = jnp.ones((8, CAP), F32)
+    lane = lax.broadcasted_iota(jnp.int32, (8, CAP), 1)
+    row = lax.broadcasted_iota(jnp.int32, (CAP, CAP), 0)
+    col = lax.broadcasted_iota(jnp.int32, (CAP, CAP), 1)
+    named = jnp.where(lane < NB, plan[...], -1)
+    held = []
+    for start in range(0, size, CAP):
+        stop = min(start + CAP, size)
+        live = jnp.where(table[start:stop, 3, :] > 0.0, 1.0, 0.0)
+        if stop - start < CAP:
+            live = jnp.concatenate([live, jnp.zeros((CAP - (stop - start), CAP), F32)], axis=0)
+        held.append(
+            lax.dot_general(ones, live, (((1,), (1,)), ((), ())), preferred_element_type=F32)
+        )
+    lines = []
+    for k in range(C_DEV):
+        line = jnp.zeros((8, CAP), F32)
+        for i, counts in enumerate(held):
+            same = jnp.where(named[k : k + 1] == row + i * CAP, 1.0, 0.0)
+            line += jnp.dot(counts, same, preferred_element_type=F32)
+        lines.append(line[0:1])
+    before = jnp.where(row < col, 1.0, 0.0)
+    return jnp.dot(jnp.concatenate(lines, axis=0), before, preferred_element_type=F32)
+
+
 def moving_kernel(
-    regions, planes, exports, energy, density, table,
-    cells, land, outbox, region_sems, along_sems, across_sems,
+    regions, planes, exports, energy, density, table_one, plan, derived, offsets,
+    table, cells, land, outbox, region_sems, along_sems, across_sems,
 ):
     wait_for_all = greet(regions, planes)
     for k in range(C_DEV):
-        cells[k, 0:1] = energy[k : k + 1]
-        cells[k, 1:2] = density[k : k + 1]
+        heat = (ADIABATIC * (ADIABATIC - 1.0)) * energy[k : k + 1]
+        cells[k, 0:1] = SOUND_UNIT * jnp.sqrt(heat)
+        cells[k, 1:2] = DENSITY_UNIT * density[k : k + 1]
     wait_for_all()
     regionals = region_copies(regions, cells, table, region_sems)
     blocks = [
@@ -246,6 +292,20 @@
     for copy in blocks + list(regionals):
         copy.start()
     choose(0, exports, cells, outbox)
+
+    def prepare(s, carry):
+        h, m = table_one[s, 4:5], table_one[s, 3:4]
+        inverse = 1.0 / h
+        second = inverse * inverse
+        derived[s, 0:1] = second
+        derived[s, 1:2] = second * inverse
+        derived[s, 2:3] = 0.05 * h
+        derived[s, 3:4] = m * (1.5 / math.pi)
+        derived[s, 7:8] = m
+        return carry
+
+    lax.fori_loop(0, table.shape[0], prepare, 0, unroll=6)
+    offsets[...] = offsets_of(table_one, plan).astype(jnp.int32)
     pltpu.make_async_copy(land, land, along_sems.at[1]).wait()
     for i in range(planes - 1):
         choose(i + 1, exports, land.at[i], outbox)
@@ -259,6 +319,14 @@
     pltpu.make_async_copy(land, land, along_sems.at[0]).wait()
     drain(planes, outbox, table, across_sems.at[0], across_sems.at[1])
 
+    def complete(s, carry):
+        sound, thin = table[s, 0:1], table[s, 1:2]
+        derived[s, 4:5] = (4.0 / ADIABATIC) * (sound * sound) / thin
+        derived[s, 5:7] = table[s]
+        return carry
+
+    lax.fori_loop(0, table.shape[0], complete, 0, unroll=6)
+
 
 def fill_shifts(shifts):
     sub = lax.broadcasted_iota(jnp.int32, (8, CAP), 0)
@@ -270,18 +338,38 @@
         )
 
 
-def wide(column):
-    return jnp.broadcast_to(column, (GROUP, CAP))
-
-
-def gather(plan, k, block_of, near):
+def pack(plan, offsets, k, blocks_of, deads, packed):
+    lane = lax.broadcasted_iota(jnp.int32, (8, CAP), 1)
+    current = deads
     for n in range(NB):
-        near[n] = block_of(plan[k, n], n)
+        at, end = offsets[k, n], offsets[k, n + 1]
+        row, first = lax.shift_right_logical(at, 7), lax.bitwise_and(at, CAP - 1)
+        kept = lane < first
+        spilled = lax.shift_right_logical(end, 7) > row
+        rolled = [pltpu.roll(block, first, 1) for block in blocks_of(plan[k, n], n)]
+        current = [jnp.where(kept, old, new) for old, new in zip(current, rolled)]
+        for ref, value in zip(packed, current):
+            ref[row] = value
+        current = [jnp.where(spilled, new, old) for old, new in zip(current, rolled)]
+    at = offsets[k, NB]
+    row, first = lax.shift_right_logical(at, 7), lax.bitwise_and(at, CAP - 1)
+    for ref, value, dead in zip(packed, current, deads):
+        ref[row] = jnp.where(lane < first, value, dead)
+        for i in range(1, 8):
+            ref[row + i] = dead
+    return lax.shift_right_logical(at + CAP - 1, 7)
+
+
+def by_size(rows, run):
+    low = 0
+    for size in SIZES:
+        pl.when(jnp.logical_and(rows > low, rows <= size))(functools.partial(run, size))
+        low = size
 
 
 def density_kernel(
-    plan, table, comp, rank, density_old,
-    density, density_too, comp_density,
+    plan, table, targets, rank, density_old,
+    density, density_too, own,
     shifts, near, total,
 ):
     fill_shifts(shifts)
@@ -289,21 +377,21 @@
     cube = 4.0 ** (-1.0 / 3.0)
 
     def cell(k, carry):
-        gather(plan, k, lambda s, n: table[s] + shifts[plan[k, SHIFT_AT + n]], near)
+        for n in range(NB):
+            near[n] = table[plan[k, n]] + shifts[plan[k, SHIFT_AT + n]]
         ranks = rank[pl.ds(k, 1), :]
         total[...] = jnp.zeros((GROUP, CAP), F32)
         groups = plan[k, GROUP_AT]
 
         def setup(g):
             at = pl.multiple_of(jnp.minimum(g, CAP // GROUP - 1) * GROUP, GROUP)
-            tile = comp[k, pl.ds(at, GROUP), :]
-            x, y, z, h = (wide(tile[:, f : f + 1]) for f in (0, 1, 2, 4))
-            return x, y, z, 1.0 / h
+            return tuple(targets[f, k, pl.ds(at, GROUP), :] for f in (X, Y, Z, INVERSE))
 
         def finish(g, partial, norm):
             found = jnp.sum(partial, axis=1, keepdims=True) * norm
             at = pl.multiple_of(jnp.maximum(g, 0) * GROUP, GROUP)
-            comp_density[k, pl.ds(at, GROUP), :] = found
+            own[0, k, pl.ds(at, GROUP), :] = targets[HEAT, k, pl.ds(at, GROUP), :] / found
+            own[1, k, pl.ds(at, GROUP), :] = jnp.broadcast_to(found, (GROUP, CAP)) * DENSITY_UNIT
             here = ranks == (sub + g * GROUP).astype(F32)
             total[...] += jnp.where(here, found, 0.0)
 
@@ -340,48 +428,29 @@
 
 
 def force_kernel(
-    plan, table, moving, comp, comp_density, rank, velocity, time_bin,
-    acceleration, kicked, shifts, near, derived, more, total,
+    plan, offsets, table, derived, targets, own, rank, velocity, time_bin,
+    acceleration, kicked, shifts, near, more, total,
 ):
     sub = lax.broadcasted_iota(jnp.int32, (GROUP, CAP), 0)
 
-    def derive(s, carry):
-        h, m = table[s, 4:5], table[s, 3:4]
-        e, rho = moving[s, 0:1], moving[s, 1:2]
-        inverse = 1.0 / h
-        second = inverse * inverse
-        derived[s, 0:1] = second
-        derived[s, 1:2] = second * inverse
-        derived[s, 2:3] = 0.05 * h
-        derived[s, 3:4] = m * (1.5 / math.pi)
-        derived[s, 4:5] = (ADIABATIC - 1.0) * e / rho
-        derived[s, 5:6] = 0.025 * jnp.sqrt(ADIABATIC * (ADIABATIC - 1.0) * e)
-        derived[s, 6:7] = rho * (1.0 / 400.0)
-        derived[s, 7:8] = rho
-        return carry
-
     fill_shifts(shifts)
-    lax.fori_loop(0, table.shape[0], derive, 0, unroll=6)
+    deads = [table[0], jnp.where(sub == 3, 0.0, derived[0])]
 
     def cell(k, carry):
-        gather(plan, k, lambda s, n: table[s] + shifts[plan[k, SHIFT_AT + n]], near)
-        gather(plan, k, lambda s, n: derived[s], more)
+        rows = pack(
+            plan, offsets, k,
+            lambda s, n: (table[s] + shifts[plan[k, SHIFT_AT + n]], derived[s]),
+            deads, (near, more),
+        )
         ranks = rank[pl.ds(k, 1), :]
         total[...] = jnp.zeros((3, GROUP, CAP), F32)
         groups = plan[k, GROUP_AT]
 
         def setup(g):
             at = pl.multiple_of(jnp.minimum(g, CAP // GROUP - 1) * GROUP, GROUP)
-            tile = comp[k, pl.ds(at, GROUP), :]
-            x, y, z, e, h, vx, vy, vz = (wide(tile[:, f : f + 1]) for f in range(8))
-            rho = comp_density[k, pl.ds(at, GROUP), :]
-            inverse = 1.0 / h
-            second = inverse * inverse
-            press = (ADIABATIC - 1.0) * e / rho
-            sound = 0.025 * jnp.sqrt(ADIABATIC * (ADIABATIC - 1.0) * e)
-            return (
-                x, y, z, vx, vy, vz, second, second * inverse, 0.05 * h, press, sound,
-                rho * (1.0 / 400.0),
+            columns = (X, Y, Z, VX, VY, VZ, SECOND, THIRD, SMALL, SOUND)
+            return tuple(targets[f, k, pl.ds(at, GROUP), :] for f in columns) + tuple(
+                own[f, k, pl.ds(at, GROUP), :] for f in range(2)
             )
 
         def finish(g, parts):
@@ -391,7 +460,7 @@
 
         def run(size):
             def group(g, carry):
-                (x, y, z, vx, vy, vz, second, third, small, press, sound, thin), parts = carry
+                (x, y, z, vx, vy, vz, second, third, small, sound, press, thin), parts = carry
                 finish(g - 1, parts)
                 following = setup(g + 1)
                 ax = ay = az = jnp.zeros((GROUP, CAP), F32)
@@ -427,7 +496,7 @@
             _, parts = lax.fori_loop(0, groups, group, (setup(0), (none, none, none)))
             finish(groups - 1, parts)
 
-        run(NB)
+        by_size(rows, run)
         mine = pl.ds(k, 1)
         step = STEP_MAX * jnp.exp2(-time_bin[mine, :].astype(F32))
         for i in range(3):
@@ -459,11 +528,11 @@
     def floats(*dims):
         return pltpu.VMEM(dims, F32)
 
-    limit = 48 << 20
-    table, comp, rank, plan, exports, energy, density_old = pl.pallas_call(
+    limit = 32 << 20
+    table, targets, rank, plan, exports, energy, density_old = pl.pallas_call(
         functools.partial(static_kernel, regions, planes),
         out_shape=[
-            shape(size, 8, CAP), shape(C_DEV, CAP, 8), shape(C_DEV, CAP),
+            shape(size, 8, CAP), shape(TARGET, C_DEV, CAP, CAP), shape(C_DEV, CAP),
             shape(C_DEV, CAP, dtype=jnp.int32),
             shape(planes, 2, planes * PLANE, dtype=jnp.int32), shape(C_DEV, CAP), shape(C_DEV, CAP),
         ],
@@ -491,38 +560,38 @@
             )
         )
     )
-    density, density_too, comp_density = pl.pallas_call(
+    density, density_too, own = pl.pallas_call(
         density_kernel,
-        out_shape=[shape(C_DEV, CAP), shape(C_DEV, CAP), shape(C_DEV, CAP, CAP)],
+        out_shape=[shape(C_DEV, CAP), shape(C_DEV, CAP), shape(2, C_DEV, CAP, CAP)],
         in_specs=[smem] + [vmem] * 4,
         out_specs=[vmem] * 3,
         scratch_shapes=[floats(NB, 8, CAP), floats(NB, 8, CAP), floats(GROUP, CAP)],
         compiler_params=pltpu.CompilerParams(vmem_limit_bytes=limit),
-    )(plan, table, comp, rank, density_old)
-    moving = pl.pallas_call(
+    )(plan, table, targets, rank, density_old)
+    derived, offsets = pl.pallas_call(
         functools.partial(moving_kernel, regions, planes),
-        out_shape=shape(size, 2, CAP),
-        in_specs=[smem, vmem, vmem],
-        out_specs=vmem,
+        out_shape=[shape(size, 8, CAP), shape(C_DEV, CAP, dtype=jnp.int32)],
+        in_specs=[smem] + [vmem] * 4,
+        out_specs=[vmem] * 2,
         scratch_shapes=[
-            floats(C_DEV, 2, CAP), floats(planes - 1, C_DEV, 2, CAP),
+            floats(size, 2, CAP), floats(C_DEV, 2, CAP), floats(planes - 1, C_DEV, 2, CAP),
             floats(PLANE, 2 * planes, 2, CAP), dma((4,)), dma((2,)), dma((2,)),
         ],
         compiler_params=pltpu.CompilerParams(
             collective_id=1, has_side_effects=True, vmem_limit_bytes=limit
         ),
-    )(exports, energy, density_too)
+    )(exports, energy, density_too, table, plan)
     acceleration, kicked = pl.pallas_call(
         force_kernel,
         out_shape=[shape(3, C_DEV, CAP), shape(3, C_DEV, CAP)],
-        in_specs=[smem] + [vmem] * 7,
+        in_specs=[smem] * 2 + [vmem] * 7,
         out_specs=[vmem, vmem],
         scratch_shapes=[
-            floats(NB, 8, CAP), floats(NB, 8, CAP), floats(size, 8, CAP), floats(NB, 8, CAP),
+            floats(NB, 8, CAP), floats(ROWS, 8, CAP), floats(ROWS, 8, CAP),
             floats(3, GROUP, CAP),
         ],
         compiler_params=pltpu.CompilerParams(vmem_limit_bytes=limit),
-    )(plan, table, moving, comp, comp_density, rank, velocity, time_bin)
+    )(plan, offsets, table, derived, targets, own, rank, velocity, time_bin)
     return density, acceleration, kicked
 
 

time: 56.3 us -> 55.8 us (level)
  the two profiles are of different devices: /device:TPU:49 before, /device:TPU:7 now
where the time goes in v3:
time: 55.8 us; the launch traced here: 55.6 us
  Pallas kernels  54.9 us (98%)
  between operations  0.68 us (1%)
    pallas_call x1, Pallas kernels, shards(): pl.pallas_call(functools.partial(static_kernel, regions, planes), out_sha...  24.6 us
    pallas_call x1, Pallas kernels, shards(): pl.pallas_call(functools.partial(moving_kernel, regions, planes), out_sha...  13.8 us
    pallas_call x1, Pallas kernels, shards(): pl.pallas_call(force_kernel, out_shape=[shape(3, C_DEV, CAP), shape(3, C_...  10.6 us
    pallas_call x1, Pallas kernels, shards(): pl.pallas_call(density_kernel, out_shape=[shape(C_DEV, CAP), shape(C_DEV,...  5.98 us

profile of v3, /device:TPU:7, one launch (start us, length us, event | category | flops | bytes accessed | tf_op | source)
XLA Modules:
  0.0 55.6 jit_solution(14138045224217632039)
XLA Ops:
  0.6 0.0 copy-start
  0.6 0.0 copy-start.1
  0.7 24.6 %shard_map.139 = (f32[138,8,128]{2,1,0:T(8,128)S(1)}, f32[12,8,128,128]{3,2,1,0:T(8,128)S(1)}, f32[8,128]{1,0:T(8,128)S(1)}, s32[8,128]{1,0:T(8,128)S(1)}, s32[8...) custom-call(f32[3,8,128]{2,1,0:T(8,128)} %position.1, f32[3,8,128]{2,1,0:T(8,128)} %velocity.3, ...), custom_call_target="tpu_custom_call" | custom-call | tf_op jit(solution)/shard_map/pallas_call | solution.py:532
  25.3 6.0 %shard_map.140 = (f32[8,128]{1,0:T(8,128)}, f32[8,128]{1,0:T(8,128)S(1)}, f32[2,8,128,128]{3,2,1,0:T(8,128)S(1)}) custom-call(s32[8,128]{1,0:T(8,128)S(1)} %get-tuple-element.17.plan, f32[138,8,128]{2,1,0:T(8,128)S(1)} %get-tuple-element.18.table.table_one, f32[12,8,128,128]{3,2,1,0:T(8,128)S(1)} %get-tuple-element.19.targets, ...), custom_call_target="tpu_custom_call" | custom-call | tf_op jit(solution)/shard_map/pallas_call | solution.py:563
  31.2 13.8 %shard_map.141 = (f32[138,8,128]{2,1,0:T(8,128)S(1)}, s32[8,128]{1,0:T(8,128)S(1)}) custom-call(s32[8,2,64]{2,1,0:T(2,128)S(1)} %get-tuple-element.23.exports, f32[8,128]{1,0:T(8,128)S(1)} %get-tuple-element.24.energy, f32[8,128]{1,0:T(8,128)S(1)} %get-tuple-element.25.density, f32[138,8,128]{2,1,0:T(8,128)S(1)} %get-tuple-element.18.table.table_one, ...), custom_call_target="tpu_custom_call" | custom-call | tf_op jit(solution)/shard_map/pallas_call | solution.py:571
  45.0 0.0 copy-done
  45.0 0.0 copy-done.1
  45.0 10.6 %shard_map.142 = (f32[3,8,128]{2,1,0:T(8,128)}, f32[3,8,128]{2,1,0:T(8,128)}) custom-call(s32[8,128]{1,0:T(8,128)S(1)} %get-tuple-element.17.plan, s32[8,128]{1,0:T(8,128)S(1)} %get-tuple-element.26.offsets, f32[138,8,128]{2,1,0:T(8,128)S(1)} %get-tuple-element.18.table.table_one, f32[138,8,128]{2,1,0:T(8,128)S(1)} %get-tuple-element.27.derived, ...), custom_call_target="tpu_custom_call" | custom-call | tf_op jit(solution)/shard_map/pallas_call | solution.py:584
Async XLA Ops:
  0.6 44.4 %copy-start = (f32[3,8,128]{2,1,0:T(8,128)S(1)}, f32[3,8,128]{2,1,0:T(8,128)}, u32[]{:S(2)}) copy-start(f32[3,8,128]{2,1,0:T(8,128)} %velocity.3) | copy-start | bytes 36868
  0.6 44.4 %copy-start.1 = (s32[8,128]{1,0:T(8,128)S(1)}, s32[8,128]{1,0:T(8,128)}, u32[]{:S(2)}) copy-start(s32[8,128]{1,0:T(8,128)} %time_bin.1) | copy-start | bytes 12292

commit v4 on v3

--- a/solution.py
+++ b/solution.py
@@ -15,6 +15,7 @@
 GROUP = 8
 PLANE = 8
 ORDER = (1, 7, 4, 2, 6, 3, 5)
+EARLY = 6
 BATCH = 2
 ADIABATIC = 5.0 / 3.0
 STEP_MAX = 0.2
@@ -61,22 +62,22 @@
     return lambda: pl.semaphore_wait(barrier, planes + PLANE)
 
 
-def region_copies(regions, cells, table, sems):
+def region_copies(regions, cells, table, sems, first):
     r, z, u = place()
     size = table.shape[0]
     up = pltpu.make_async_remote_copy(
         src_ref=cells.at[pl.ds(C_DEV - 1, 1)],
         dst_ref=table.at[pl.ds(size - 2, 1)],
-        send_sem=sems.at[0],
-        recv_sem=sems.at[1],
+        send_sem=sems.at[first + 0],
+        recv_sem=sems.at[first + 1],
         device_id=(lax.rem(r + 1, regions), z * PLANE + u),
         device_id_type=MESH,
     )
     down = pltpu.make_async_remote_copy(
         src_ref=cells.at[pl.ds(0, 1)],
         dst_ref=table.at[pl.ds(size - 1, 1)],
-        send_sem=sems.at[2],
-        recv_sem=sems.at[3],
+        send_sem=sems.at[first + 2],
+        recv_sem=sems.at[first + 3],
         device_id=(lax.rem(r + regions - 1, regions), z * PLANE + u),
         device_id_type=MESH,
     )
@@ -91,15 +92,15 @@
     )
 
 
-def send_across(first, cells, outbox, table, send_sem, recv_sem):
-    r, z, u = place()
-    rows = 2 * BATCH
+def send_across(first, slots, planes, outbox, table, send_sem, recv_sem):
+    r, z, u = place()
+    rows = 2 * slots
 
     def send(ahead, carry):
         to = lax.rem(u + ahead, PLANE)
         pltpu.make_async_remote_copy(
             src_ref=outbox.at[to, pl.ds(2 * first, rows)],
-            dst_ref=table.at[pl.ds(C_DEV + 2 * cells * u + 2 * first, rows)],
+            dst_ref=table.at[pl.ds(C_DEV + 2 * planes * u + 2 * first, rows)],
             send_sem=send_sem, recv_sem=recv_sem,
             device_id=(r, z * PLANE + to), device_id_type=MESH,
         ).start()
@@ -137,13 +138,15 @@
 def static_kernel(
     regions, planes,
     position, velocity, smoothing, mass, energy, active, count, export, source, shift, old,
-    table, targets, rank, plan, exports, energy_v, old_v,
-    position_v, velocity_v, smoothing_v, mass_v, active_v, count_s, source_v, shift_v,
+    table, sounds, targets, rank, plan, exports, old_v,
+    energy_v, position_v, velocity_v, smoothing_v, mass_v, active_v, count_s, source_v, shift_v,
     cells, exports_s, outbox, *rest,
 ):
-    land, (fetch_sems, region_sems, export_sems, along_send, along_recv, across_sems, own_sem) = (
-        rest[: planes - 1], rest[planes - 1 :]
-    )
+    land, (
+        sound_land, sound_outbox,
+        fetch_sems, region_sems, export_sems, along_send, along_recv, across_sems, own_sem,
+        sound_sems,
+    ) = rest[: planes - 1], rest[planes - 1 :]
     wait_for_all = greet(regions, planes)
     fetches = [
         pltpu.make_async_copy(a, b, fetch_sems.at[i])
@@ -164,8 +167,19 @@
             cells[k, 5 + i : 6 + i] = velocity_v[i, k : k + 1]
         cells[k, 3:4] = jnp.where(slot < count_s[k], mass_v[k : k + 1], 0.0)
         cells[k, 4:5] = smoothing_v[k : k + 1]
+        heat = (ADIABATIC * (ADIABATIC - 1.0)) * energy_v[k : k + 1]
+        sound_land[0, k] = SOUND_UNIT * jnp.sqrt(heat)
     wait_for_all()
-    regionals = region_copies(regions, cells, table, region_sems)
+    regionals = region_copies(regions, cells, table, region_sems, 0) + region_copies(
+        regions, sound_land.at[0], sounds, region_sems, 4
+    )
+    calls = [
+        send_along(
+            planes, ahead, sound_land.at[0], sound_land.at[i + 1], sound_sems.at[0],
+            sound_sems.at[1],
+        )
+        for i, ahead in enumerate(ORDER)
+    ]
     lists = [
         send_along(
             planes, ahead, exports.at[0], exports.at[i + 1], export_sems.at[0], export_sems.at[1]
@@ -176,7 +190,7 @@
         send_along(planes, ahead, cells, land[i], along_send.at[i], along_recv.at[i])
         for i, ahead in enumerate(ORDER)
     ]
-    for copy in lists + blocks[:2] + list(regionals) + blocks[2:]:
+    for copy in lists + calls + blocks[:2] + list(regionals) + blocks[2:]:
         copy.start()
 
     live = active_v[...] > 0
@@ -201,13 +215,6 @@
     plan[:, SHIFT_AT : SHIFT_AT + NB] = shift_v[...]
     plan[:, GROUP_AT : GROUP_AT + 1] = groups
 
-    drained = exports.at[pl.ds(1, planes - 1)]
-    pltpu.make_async_copy(drained, drained, export_sems.at[1]).wait()
-    pltpu.make_async_copy(drained, drained, export_sems.at[0]).wait()
-    to_scalar = pltpu.make_async_copy(exports, exports_s, own_sem)
-    to_scalar.start()
-    to_scalar.wait()
-    choose(0, exports_s, cells, outbox)
     sub = lax.broadcasted_iota(jnp.int32, (8, CAP), 0)
 
     def compact(k):
@@ -230,20 +237,37 @@
         ):
             targets[at, k] = value
 
+    for k in range(EARLY):
+        compact(k)
+    drained = exports.at[pl.ds(1, planes - 1)]
+    pltpu.make_async_copy(drained, drained, export_sems.at[1]).wait()
+    pltpu.make_async_copy(drained, drained, export_sems.at[0]).wait()
+    to_scalar = pltpu.make_async_copy(exports, exports_s, own_sem)
+    to_scalar.start()
+    to_scalar.wait()
+    heard = sound_land.at[pl.ds(1, planes - 1)]
+    pltpu.make_async_copy(heard, heard, sound_sems.at[1]).wait()
+    for slot in range(planes):
+        choose(slot, exports_s, sound_land.at[slot], sound_outbox)
+    send_across(0, planes, planes, sound_outbox, sounds, sound_sems.at[2], sound_sems.at[3])
+    choose(0, exports_s, cells, outbox)
     for i in range(planes - 1):
-        compact(i)
+        if i + EARLY < C_DEV:
+            compact(i + EARLY)
         blocks[i].wait_recv()
         choose(i + 1, exports_s, land[i], outbox)
         if (i + 2) % BATCH == 0:
             send_across(
-                i + 2 - BATCH, planes, outbox, table, across_sems.at[0], across_sems.at[1]
+                i + 2 - BATCH, BATCH, planes, outbox, table, across_sems.at[0], across_sems.at[1]
             )
-    compact(planes - 1)
     keep_own(planes, cells, outbox, table)
+    keep_own(planes, sound_land.at[0], sound_outbox, sounds)
     for copy in regionals:
         copy.wait()
     for copy in blocks:
         copy.wait_send()
+    pltpu.make_async_copy(heard, heard, sound_sems.at[0]).wait()
+    drain(planes, sound_outbox, sounds, sound_sems.at[2], sound_sems.at[3])
     drain(planes, outbox, table, across_sems.at[0], across_sems.at[1])
 
 
@@ -274,55 +298,80 @@
     return jnp.dot(jnp.concatenate(lines, axis=0), before, preferred_element_type=F32)
 
 
+def by_distance(planes):
+    others = [(i, j) for i in range(planes) for j in range(PLANE) if (i, j) != (0, 0)]
+
+    def hops(other):
+        return min(other[0], planes - other[0]) + min(other[1] // 2, (PLANE - other[1] + 1) // 2)
+
+    return sorted(others, key=lambda other: -hops(other))
+
+
 def moving_kernel(
-    regions, planes, exports, energy, density, table_one, plan, derived, offsets,
-    table, cells, land, outbox, region_sems, along_sems, across_sems,
+    regions, planes, exports, density, sources, sounds, plan, derived, offsets,
+    table, cells, outbox, region_sems, sems,
 ):
-    wait_for_all = greet(regions, planes)
+    r, z, u = place()
+    others = by_distance(planes)
+    barrier = pltpu.get_barrier_semaphore()
+
+    def at(other):
+        return lax.rem(z + other[0], planes) * PLANE + lax.rem(u + other[1], PLANE)
+
+    for other in others:
+        pl.semaphore_signal(barrier, inc=1, device_id=(r, at(other)), device_id_type=MESH)
+    for ahead in (1, regions - 1):
+        pl.semaphore_signal(
+            barrier, inc=1, device_id=(lax.rem(r + ahead, regions), z * PLANE + u),
+            device_id_type=MESH,
+        )
     for k in range(C_DEV):
-        heat = (ADIABATIC * (ADIABATIC - 1.0)) * energy[k : k + 1]
-        cells[k, 0:1] = SOUND_UNIT * jnp.sqrt(heat)
-        cells[k, 1:2] = DENSITY_UNIT * density[k : k + 1]
-    wait_for_all()
-    regionals = region_copies(regions, cells, table, region_sems)
-    blocks = [
-        send_along(planes, ahead, cells, land.at[i], along_sems.at[0], along_sems.at[1])
-        for i, ahead in enumerate(ORDER)
-    ]
-    for copy in blocks + list(regionals):
+        cells[k] = DENSITY_UNIT * density[k : k + 1]
+    for i, other in enumerate(others):
+        for q in range(2):
+            outbox[i, q] = cells[exports[0, q, at(other)]]
+    pl.semaphore_wait(barrier, planes * PLANE + 1)
+    for i, other in enumerate(others):
+        slot = ((0,) + ORDER).index(other[0])
+        pltpu.make_async_remote_copy(
+            src_ref=outbox.at[i],
+            dst_ref=table.at[pl.ds(C_DEV + 2 * planes * u + 2 * slot, 2)],
+            send_sem=sems.at[0], recv_sem=sems.at[1],
+            device_id=(r, at(other)), device_id_type=MESH,
+        ).start()
+    regionals = region_copies(regions, cells, table, region_sems, 0)
+    for copy in regionals:
         copy.start()
-    choose(0, exports, cells, outbox)
+    for k in range(C_DEV):
+        table[k] = cells[k]
+    for q in range(2):
+        table[C_DEV + 2 * planes * u + q] = cells[exports[0, q, z * PLANE + u]]
 
     def prepare(s, carry):
-        h, m = table_one[s, 4:5], table_one[s, 3:4]
+        h, m = sources[s, 4:5], sources[s, 3:4]
         inverse = 1.0 / h
         second = inverse * inverse
         derived[s, 0:1] = second
         derived[s, 1:2] = second * inverse
         derived[s, 2:3] = 0.05 * h
         derived[s, 3:4] = m * (1.5 / math.pi)
-        derived[s, 7:8] = m
+        sound = sounds[s]
+        derived[s, 5:6] = sound
+        derived[s, 7:8] = (4.0 / ADIABATIC) * (sound * sound)
         return carry
 
     lax.fori_loop(0, table.shape[0], prepare, 0, unroll=6)
-    offsets[...] = offsets_of(table_one, plan).astype(jnp.int32)
-    pltpu.make_async_copy(land, land, along_sems.at[1]).wait()
-    for i in range(planes - 1):
-        choose(i + 1, exports, land.at[i], outbox)
-        if (i + 2) % BATCH == 0:
-            send_across(
-                i + 2 - BATCH, planes, outbox, table, across_sems.at[0], across_sems.at[1]
-            )
-    keep_own(planes, cells, outbox, table)
+    offsets[...] = offsets_of(sources, plan).astype(jnp.int32)
     for copy in regionals:
         copy.wait()
-    pltpu.make_async_copy(land, land, along_sems.at[0]).wait()
-    drain(planes, outbox, table, across_sems.at[0], across_sems.at[1])
+    pltpu.make_async_copy(outbox, outbox, sems.at[0]).wait()
+    landed = table.at[pl.ds(0, 2 * len(others))]
+    pltpu.make_async_copy(landed, landed, sems.at[1]).wait()
 
     def complete(s, carry):
-        sound, thin = table[s, 0:1], table[s, 1:2]
-        derived[s, 4:5] = (4.0 / ADIABATIC) * (sound * sound) / thin
-        derived[s, 5:7] = table[s]
+        thin = table[s]
+        derived[s, 4:5] = derived[s, 7:8] / thin
+        derived[s, 6:7] = thin
         return carry
 
     lax.fori_loop(0, table.shape[0], complete, 0, unroll=6)
@@ -529,24 +578,26 @@
         return pltpu.VMEM(dims, F32)
 
     limit = 32 << 20
-    table, targets, rank, plan, exports, energy, density_old = pl.pallas_call(
+    table, sounds, targets, rank, plan, exports, density_old = pl.pallas_call(
         functools.partial(static_kernel, regions, planes),
         out_shape=[
-            shape(size, 8, CAP), shape(TARGET, C_DEV, CAP, CAP), shape(C_DEV, CAP),
+            shape(size, 8, CAP), shape(size, 1, CAP), shape(TARGET, C_DEV, CAP, CAP),
+            shape(C_DEV, CAP),
             shape(C_DEV, CAP, dtype=jnp.int32),
-            shape(planes, 2, planes * PLANE, dtype=jnp.int32), shape(C_DEV, CAP), shape(C_DEV, CAP),
+            shape(planes, 2, planes * PLANE, dtype=jnp.int32), shape(C_DEV, CAP),
         ],
         in_specs=[hbm] * 11,
         out_specs=[vmem] * 7,
         scratch_shapes=[
-            floats(3, C_DEV, CAP), floats(3, C_DEV, CAP), floats(C_DEV, CAP), floats(C_DEV, CAP),
-            ints(C_DEV, CAP), pltpu.SMEM((C_DEV,), jnp.int32),
+            floats(C_DEV, CAP), floats(3, C_DEV, CAP), floats(3, C_DEV, CAP), floats(C_DEV, CAP),
+            floats(C_DEV, CAP), ints(C_DEV, CAP), pltpu.SMEM((C_DEV,), jnp.int32),
             ints(C_DEV, NB), ints(C_DEV, NB),
             floats(C_DEV, 8, CAP), pltpu.SMEM((planes, 2, planes * PLANE), jnp.int32),
             floats(PLANE, 2 * planes, 8, CAP),
             *[floats(C_DEV, 8, CAP) for _ in range(planes - 1)],
-            dma((11,)), dma((4,)), dma((2,)), dma((planes - 1,)), dma((planes - 1,)), dma((2,)),
-            dma,
+            floats(planes, C_DEV, 1, CAP), floats(PLANE, 2 * planes, 1, CAP),
+            dma((11,)), dma((8,)), dma((2,)), dma((planes - 1,)), dma((planes - 1,)), dma((2,)),
+            dma, dma((4,)),
         ],
         compiler_params=pltpu.CompilerParams(
             collective_id=0, has_side_effects=True, vmem_limit_bytes=limit
@@ -574,13 +625,13 @@
         in_specs=[smem] + [vmem] * 4,
         out_specs=[vmem] * 2,
         scratch_shapes=[
-            floats(size, 2, CAP), floats(C_DEV, 2, CAP), floats(planes - 1, C_DEV, 2, CAP),
-            floats(PLANE, 2 * planes, 2, CAP), dma((4,)), dma((2,)), dma((2,)),
+            floats(size, 1, CAP), floats(C_DEV, 1, CAP),
+            floats(planes * PLANE - 1, 2, 1, CAP), dma((4,)), dma((2,)),
         ],
         compiler_params=pltpu.CompilerParams(
             collective_id=1, has_side_effects=True, vmem_limit_bytes=limit
         ),
-    )(exports, energy, density_too, table, plan)
+    )(exports, density_too, table, sounds, plan)
     acceleration, kicked = pl.pallas_call(
         force_kernel,
         out_shape=[shape(3, C_DEV, CAP), shape(3, C_DEV, CAP)],

time: 55.8 us -> 54.1 us (0.970)
  the two profiles are of different devices: /device:TPU:7 before, /device:TPU:49 now
where the time goes in v4:
time: 54.1 us; the launch traced here: 53.9 us
  Pallas kernels  53.2 us (98%)
  between operations  0.68 us (1%)
    pallas_call x1, Pallas kernels, shards(): pl.pallas_call(functools.partial(static_kernel, regions, planes), out_sha...  25.5 us
    pallas_call x1, Pallas kernels, shards(): pl.pallas_call(functools.partial(moving_kernel, regions, planes), out_sha...  11.3 us
    pallas_call x1, Pallas kernels, shards(): pl.pallas_call(force_kernel, out_shape=[shape(3, C_DEV, CAP), shape(3, C_...  10.2 us
    pallas_call x1, Pallas kernels, shards(): pl.pallas_call(density_kernel, out_shape=[shape(C_DEV, CAP), shape(C_DEV,...  6.08 us

profile of v4, /device:TPU:49, one launch (start us, length us, event | category | flops | bytes accessed | tf_op | source)
XLA Modules:
  0.0 53.9 jit_solution(177344614803904101)
XLA Ops:
  0.6 0.0 copy-start
  0.6 0.0 copy-start.1
  0.7 25.5 %shard_map.139 = (f32[138,8,128]{2,1,0:T(8,128)S(1)}, f32[138,1,128]{2,1,0:T(1,128)S(1)}, f32[12,8,128,128]{3,2,1,0:T(8,128)S(1)}, f32[8,128]{1,0:T(8,128)S(1)},...) custom-call(f32[3,8,128]{2,1,0:T(8,128)} %position.1, f32[3,8,128]{2,1,0:T(8,128)} %velocity.3, ...), custom_call_target="tpu_custom_call" | custom-call | tf_op jit(solution)/shard_map/pallas_call | solution.py:581
  26.2 6.1 %shard_map.140 = (f32[8,128]{1,0:T(8,128)}, f32[8,128]{1,0:T(8,128)S(1)}, f32[2,8,128,128]{3,2,1,0:T(8,128)S(1)}) custom-call(s32[8,128]{1,0:T(8,128)S(1)} %get-tuple-element.17.plan, f32[138,8,128]{2,1,0:T(8,128)S(1)} %get-tuple-element.18.table.sources, f32[12,8,128,128]{3,2,1,0:T(8,128)S(1)} %get-tuple-element.19.targets, ...), custom_call_target="tpu_custom_call" | custom-call | tf_op jit(solution)/shard_map/pallas_call | solution.py:614
  32.3 11.3 %shard_map.141 = (f32[138,8,128]{2,1,0:T(8,128)S(1)}, s32[8,128]{1,0:T(8,128)S(1)}) custom-call(s32[8,2,64]{2,1,0:T(2,128)S(1)} %get-tuple-element.23.exports, f32[8,128]{1,0:T(8,128)S(1)} %get-tuple-element.24.density, f32[138,8,128]{2,1,0:T(8,128)S(1)} %get-tuple-element.18.table.sources, f32[138,1,128]{2,1,0:T(1,128)S(1)} %get-tuple-element.25.sounds, ...), custom_call_target="tpu_custom_call" | custom-call | tf_op jit(solution)/shard_map/pallas_call | solution.py:622
  43.6 0.0 copy-done
  43.6 0.0 copy-done.1
  43.6 10.2 %shard_map.142 = (f32[3,8,128]{2,1,0:T(8,128)}, f32[3,8,128]{2,1,0:T(8,128)}) custom-call(s32[8,128]{1,0:T(8,128)S(1)} %get-tuple-element.17.plan, s32[8,128]{1,0:T(8,128)S(1)} %get-tuple-element.26.offsets, f32[138,8,128]{2,1,0:T(8,128)S(1)} %get-tuple-element.18.table.sources, f32[138,8,128]{2,1,0:T(8,128)S(1)} %get-tuple-element.27.derived, ...), custom_call_target="tpu_custom_call" | custom-call | tf_op jit(solution)/shard_map/pallas_call | solution.py:635
Async XLA Ops:
  0.6 43.0 %copy-start = (f32[3,8,128]{2,1,0:T(8,128)S(1)}, f32[3,8,128]{2,1,0:T(8,128)}, u32[]{:S(2)}) copy-start(f32[3,8,128]{2,1,0:T(8,128)} %velocity.3) | copy-start | bytes 36868
  0.6 43.0 %copy-start.1 = (s32[8,128]{1,0:T(8,128)S(1)}, s32[8,128]{1,0:T(8,128)}, u32[]{:S(2)}) copy-start(s32[8,128]{1,0:T(8,128)} %time_bin.1) | copy-start | bytes 12292

commit v5 on v4

--- a/solution.py
+++ b/solution.py
@@ -409,91 +409,113 @@
     return lax.shift_right_logical(at + CAP - 1, 7)
 
 
-def by_size(rows, run):
-    low = 0
-    for size in SIZES:
-        pl.when(jnp.logical_and(rows > low, rows <= size))(functools.partial(run, size))
-        low = size
+def by_size(rows, run, sizes=SIZES):
+    if len(sizes) == 1:
+        run(sizes[0])
+        return
+    half = len(sizes) // 2
+    fits = rows <= sizes[half - 1]
+    pl.when(fits)(lambda: by_size(rows, run, sizes[:half]))
+    pl.when(jnp.logical_not(fits))(lambda: by_size(rows, run, sizes[half:]))
 
 
 def density_kernel(
     plan, table, targets, rank, density_old,
-    density, density_too, own,
-    shifts, near, total,
+    density, own,
+    shifts, near, total, left,
 ):
     fill_shifts(shifts)
     sub = lax.broadcasted_iota(jnp.int32, (GROUP, CAP), 0)
     cube = 4.0 ** (-1.0 / 3.0)
+    none = jnp.zeros((GROUP, CAP), F32)
+    total[...] = none
+    left[0] = left[1] = none
+
+    def finish(k, g, partial, norm):
+        found = jnp.sum(partial, axis=1, keepdims=True) * norm
+        at = pl.multiple_of(jnp.maximum(g, 0) * GROUP, GROUP)
+        own[0, k, pl.ds(at, GROUP), :] = targets[HEAT, k, pl.ds(at, GROUP), :] / found
+        own[1, k, pl.ds(at, GROUP), :] = jnp.broadcast_to(found, (GROUP, CAP)) * DENSITY_UNIT
+        here = rank[pl.ds(k, 1), :] == (sub + g * GROUP).astype(F32)
+        return jnp.where(here, found, 0.0)
+
+    def settle(k):
+        last = finish(k, plan[k, GROUP_AT] - 1, left[0], left[1])
+        summed = jnp.sum(total[...] + last, axis=0, keepdims=True)
+        mine = pl.ds(k, 1)
+        density[mine, :] = jnp.where(rank[mine, :] >= 0.0, summed, density_old[mine, :])
+        total[...] = none
 
     def cell(k, carry):
+        settle(jnp.maximum(k - 1, 0))
         for n in range(NB):
             near[n] = table[plan[k, n]] + shifts[plan[k, SHIFT_AT + n]]
-        ranks = rank[pl.ds(k, 1), :]
-        total[...] = jnp.zeros((GROUP, CAP), F32)
-        groups = plan[k, GROUP_AT]
 
         def setup(g):
             at = pl.multiple_of(jnp.minimum(g, CAP // GROUP - 1) * GROUP, GROUP)
             return tuple(targets[f, k, pl.ds(at, GROUP), :] for f in (X, Y, Z, INVERSE))
 
-        def finish(g, partial, norm):
-            found = jnp.sum(partial, axis=1, keepdims=True) * norm
-            at = pl.multiple_of(jnp.maximum(g, 0) * GROUP, GROUP)
-            own[0, k, pl.ds(at, GROUP), :] = targets[HEAT, k, pl.ds(at, GROUP), :] / found
-            own[1, k, pl.ds(at, GROUP), :] = jnp.broadcast_to(found, (GROUP, CAP)) * DENSITY_UNIT
-            here = ranks == (sub + g * GROUP).astype(F32)
-            total[...] += jnp.where(here, found, 0.0)
-
-        def run(size):
-            def group(g, carry):
-                (x, y, z, inverse), partial, norm = carry
-                finish(g - 1, partial, norm)
-                following = setup(g + 1)
-                scaled = cube * inverse
-                partial = jnp.zeros((GROUP, CAP), F32)
-                for n in range(size):
-                    dx, dy, dz = x - near[n, 0:1], y - near[n, 1:2], z - near[n, 2:3]
-                    square = jnp.maximum(dx * dx + dy * dy + dz * dz, TINY)
-                    radius = square * lax.rsqrt(square)
-                    outer = jnp.maximum(2.0 * cube - radius * scaled, 0.0)
-                    inner = jnp.maximum(1.0 - radius * inverse, 0.0)
-                    value = outer * outer * outer - inner * inner * inner
-                    partial += near[n, 3:4] * value
-                return following, partial, inverse * inverse * inverse * (1.0 / math.pi)
-
-            none = jnp.zeros((GROUP, CAP), F32)
-            _, partial, norm = lax.fori_loop(0, groups, group, (setup(0), none, none))
-            finish(groups - 1, partial, norm)
-
-        run(NB)
-        summed = jnp.sum(total[...], axis=0, keepdims=True)
-        mine = pl.ds(k, 1)
-        found = jnp.where(ranks >= 0.0, summed, density_old[mine, :])
-        density[mine, :] = found
-        density_too[mine, :] = found
+        def group(g, carry):
+            (x, y, z, inverse), partial, norm = carry
+            total[...] += finish(k, g - 1, partial, norm)
+            following = setup(g + 1)
+            scaled = cube * inverse
+            partial = none
+            for n in range(NB):
+                dx, dy, dz = x - near[n, 0:1], y - near[n, 1:2], z - near[n, 2:3]
+                square = jnp.maximum(dx * dx + dy * dy + dz * dz, TINY)
+                radius = square * lax.rsqrt(square)
+                outer = jnp.maximum(2.0 * cube - radius * scaled, 0.0)
+                inner = jnp.maximum(1.0 - radius * inverse, 0.0)
+                value = outer * outer * outer - inner * inner * inner
+                partial += near[n, 3:4] * value
+            return following, partial, inverse * inverse * inverse * (1.0 / math.pi)
+
+        _, left[0], left[1] = lax.fori_loop(
+            0, plan[k, GROUP_AT], group, (setup(0), none, none)
+        )
         return carry
 
     lax.fori_loop(0, C_DEV, cell, 0)
+    settle(C_DEV - 1)
 
 
 def force_kernel(
-    plan, offsets, table, derived, targets, own, rank, velocity, time_bin,
-    acceleration, kicked, shifts, near, more, total,
+    plan, offsets, table, derived, targets, own, rank, velocity, time_bin, density_in,
+    acceleration, kicked, density, shifts, near, more, total, left,
 ):
+    density[...] = density_in[...]
     sub = lax.broadcasted_iota(jnp.int32, (GROUP, CAP), 0)
+    none = jnp.zeros((GROUP, CAP), F32)
+    for i in range(3):
+        total[i] = left[i] = none
 
     fill_shifts(shifts)
     deads = [table[0], jnp.where(sub == 3, 0.0, derived[0])]
 
+    def finish(k, g, parts):
+        here = rank[pl.ds(k, 1), :] == (sub + g * GROUP).astype(F32)
+        return [
+            jnp.where(here, jnp.sum(part, axis=1, keepdims=True), 0.0) for part in parts
+        ]
+
+    def settle(k):
+        last = finish(k, plan[k, GROUP_AT] - 1, [left[i] for i in range(3)])
+        mine = pl.ds(k, 1)
+        step = STEP_MAX * jnp.exp2(-time_bin[mine, :].astype(F32))
+        for i in range(3):
+            found = jnp.sum(total[i] + last[i], axis=0, keepdims=True)
+            acceleration[i, mine, :] = found
+            kicked[i, mine, :] = velocity[i, mine, :] + found * step
+            total[i] = none
+
     def cell(k, carry):
+        settle(jnp.maximum(k - 1, 0))
         rows = pack(
             plan, offsets, k,
             lambda s, n: (table[s] + shifts[plan[k, SHIFT_AT + n]], derived[s]),
             deads, (near, more),
         )
-        ranks = rank[pl.ds(k, 1), :]
-        total[...] = jnp.zeros((3, GROUP, CAP), F32)
-        groups = plan[k, GROUP_AT]
 
         def setup(g):
             at = pl.multiple_of(jnp.minimum(g, CAP // GROUP - 1) * GROUP, GROUP)
@@ -502,15 +524,11 @@
                 own[f, k, pl.ds(at, GROUP), :] for f in range(2)
             )
 
-        def finish(g, parts):
-            here = ranks == (sub + g * GROUP).astype(F32)
-            for i in range(3):
-                total[i] += jnp.where(here, jnp.sum(parts[i], axis=1, keepdims=True), 0.0)
-
         def run(size):
             def group(g, carry):
                 (x, y, z, vx, vy, vz, second, third, small, sound, press, thin), parts = carry
-                finish(g - 1, parts)
+                for i, found in enumerate(finish(k, g - 1, parts)):
+                    total[i] += found
                 following = setup(g + 1)
                 ax = ay = az = jnp.zeros((GROUP, CAP), F32)
                 for n in range(size):
@@ -541,20 +559,17 @@
                     az += weight * dz
                 return following, (ax, ay, az)
 
-            none = jnp.zeros((GROUP, CAP), F32)
-            _, parts = lax.fori_loop(0, groups, group, (setup(0), (none, none, none)))
-            finish(groups - 1, parts)
+            _, parts = lax.fori_loop(
+                0, plan[k, GROUP_AT], group, (setup(0), (none, none, none))
+            )
+            for i in range(3):
+                left[i] = parts[i]
 
         by_size(rows, run)
-        mine = pl.ds(k, 1)
-        step = STEP_MAX * jnp.exp2(-time_bin[mine, :].astype(F32))
-        for i in range(3):
-            found = jnp.sum(total[i], axis=0, keepdims=True)
-            acceleration[i, mine, :] = found
-            kicked[i, mine, :] = velocity[i, mine, :] + found * step
         return carry
 
     lax.fori_loop(0, C_DEV, cell, 0)
+    settle(C_DEV - 1)
 
 
 def shards(
@@ -611,12 +626,14 @@
             )
         )
     )
-    density, density_too, own = pl.pallas_call(
+    density, own = pl.pallas_call(
         density_kernel,
-        out_shape=[shape(C_DEV, CAP), shape(C_DEV, CAP), shape(2, C_DEV, CAP, CAP)],
+        out_shape=[shape(C_DEV, CAP), shape(2, C_DEV, CAP, CAP)],
         in_specs=[smem] + [vmem] * 4,
-        out_specs=[vmem] * 3,
-        scratch_shapes=[floats(NB, 8, CAP), floats(NB, 8, CAP), floats(GROUP, CAP)],
+        out_specs=[vmem] * 2,
+        scratch_shapes=[
+            floats(NB, 8, CAP), floats(NB, 8, CAP), floats(GROUP, CAP), floats(2, GROUP, CAP),
+        ],
         compiler_params=pltpu.CompilerParams(vmem_limit_bytes=limit),
     )(plan, table, targets, rank, density_old)
     derived, offsets = pl.pallas_call(
@@ -631,18 +648,18 @@
         compiler_params=pltpu.CompilerParams(
             collective_id=1, has_side_effects=True, vmem_limit_bytes=limit
         ),
-    )(exports, density_too, table, sounds, plan)
-    acceleration, kicked = pl.pallas_call(
+    )(exports, density, table, sounds, plan)
+    acceleration, kicked, density = pl.pallas_call(
         force_kernel,
-        out_shape=[shape(3, C_DEV, CAP), shape(3, C_DEV, CAP)],
-        in_specs=[smem] * 2 + [vmem] * 7,
-        out_specs=[vmem, vmem],
+        out_shape=[shape(3, C_DEV, CAP), shape(3, C_DEV, CAP), shape(C_DEV, CAP)],
+        in_specs=[smem] * 2 + [vmem] * 8,
+        out_specs=[vmem] * 3,
         scratch_shapes=[
             floats(NB, 8, CAP), floats(ROWS, 8, CAP), floats(ROWS, 8, CAP),
-            floats(3, GROUP, CAP),
+            floats(3, GROUP, CAP), floats(3, GROUP, CAP),
         ],
         compiler_params=pltpu.CompilerParams(vmem_limit_bytes=limit),
-    )(plan, offsets, table, derived, targets, own, rank, velocity, time_bin)
+    )(plan, offsets, table, derived, targets, own, rank, velocity, time_bin, density)
     return density, acceleration, kicked
 
 

time: 54.1 us -> 50.4 us (0.932)
  the two profiles are of different devices: /device:TPU:49 before, /device:TPU:57 now
where the time goes in v5:
time: 50.4 us; the launch traced here: 49.9 us
  Pallas kernels  49.2 us (98%)
  between operations  0.68 us (1%)
    pallas_call x1, Pallas kernels, shards(): pl.pallas_call(functools.partial(static_kernel, regions, planes), out_sha...  25.5 us
    pallas_call x1, Pallas kernels, shards(): pl.pallas_call(functools.partial(moving_kernel, regions, planes), out_sha...  12 us
    pallas_call x1, Pallas kernels, shards(): pl.pallas_call(force_kernel, out_shape=[shape(3, C_DEV, CAP), shape(3, C_...  7.74 us
    pallas_call x1, Pallas kernels, shards(): pl.pallas_call(density_kernel, out_shape=[shape(C_DEV, CAP), shape(2, C_D...  4 us

profile of v5, /device:TPU:57, one launch (start us, length us, event | category | flops | bytes accessed | tf_op | source)
XLA Modules:
  0.0 49.9 jit_solution(13161679072533775199)
XLA Ops:
  0.6 0.0 copy-start
  0.6 0.0 copy-start.1
  0.7 25.5 %shard_map.139 = (f32[138,8,128]{2,1,0:T(8,128)S(1)}, f32[138,1,128]{2,1,0:T(1,128)S(1)}, f32[12,8,128,128]{3,2,1,0:T(8,128)S(1)}, f32[8,128]{1,0:T(8,128)S(1)},...) custom-call(f32[3,8,128]{2,1,0:T(8,128)} %position.1, f32[3,8,128]{2,1,0:T(8,128)} %velocity.3, ...), custom_call_target="tpu_custom_call" | custom-call | tf_op jit(solution)/shard_map/pallas_call | solution.py:596
  26.2 4.0 %shard_map.140 = (f32[8,128]{1,0:T(8,128)S(1)}, f32[2,8,128,128]{3,2,1,0:T(8,128)S(1)}) custom-call(s32[8,128]{1,0:T(8,128)S(1)} %get-tuple-element.17.plan, f32[138,8,128]{2,1,0:T(8,128)S(1)} %get-tuple-element.19.table.sources, f32[12,8,128,128]{3,2,1,0:T(8,128)S(1)} %get-tuple-element.20.targets, f32[8,128]{1,0:T(8,128)S(1)} %get-tuple-element.21.rank, ...), custom_call_target="tpu_custom_call" | custom-call | tf_op jit(solution)/shard_map/pallas_call | solution.py:629
  30.2 12.0 %shard_map.141 = (f32[138,8,128]{2,1,0:T(8,128)S(1)}, s32[8,128]{1,0:T(8,128)S(1)}) custom-call(s32[8,2,64]{2,1,0:T(2,128)S(1)} %get-tuple-element.18.exports, f32[8,128]{1,0:T(8,128)S(1)} %get-tuple-element.23.density.density_in, f32[138,8,128]{2,1,0:T(8,128)S(1)} %get-tuple-element.19.table.sources, f32[138,1,128]{2,1,0:T(1,128)S(1)} %get-tuple-element.24.sounds, ...), custom_call_target="tpu_custom_call" | custom-call | tf_op jit(solution)/shard_map/pallas_call | solution.py:639
  42.2 0.0 copy-done
  42.2 0.0 copy-done.1
  42.2 7.7 %shard_map.142 = (f32[3,8,128]{2,1,0:T(8,128)}, f32[3,8,128]{2,1,0:T(8,128)}, f32[8,128]{1,0:T(8,128)}) custom-call(s32[8,128]{1,0:T(8,128)S(1)} %get-tuple-element.17.plan, s32[8,128]{1,0:T(8,128)S(1)} %get-tuple-element.25.offsets, f32[138,8,128]{2,1,0:T(8,128)S(1)} %get-tuple-element.19.table.sources, f32[138,8,128]{2,1,0:T(8,128)S(1)} %get-tuple-element.26.derived, ...), custom_call_target="tpu_custom_call" | custom-call | tf_op jit(solution)/shard_map/pallas_call | solution.py:652
Async XLA Ops:
  0.6 41.5 %copy-start = (f32[3,8,128]{2,1,0:T(8,128)S(1)}, f32[3,8,128]{2,1,0:T(8,128)}, u32[]{:S(2)}) copy-start(f32[3,8,128]{2,1,0:T(8,128)} %velocity.3) | copy-start | bytes 36868
  0.6 41.5 %copy-start.1 = (s32[8,128]{1,0:T(8,128)S(1)}, s32[8,128]{1,0:T(8,128)}, u32[]{:S(2)}) copy-start(s32[8,128]{1,0:T(8,128)} %time_bin.1) | copy-start | bytes 12292

commit v6 on v5

--- a/solution.py
+++ b/solution.py
@@ -46,7 +46,7 @@
 def greet(regions, planes):
     r, z, u = place()
     barrier = pltpu.get_barrier_semaphore()
-    for ahead in range(1, planes):
+    for ahead in sorted(range(1, planes), key=lambda a: -min(a, planes - a)):
         pl.semaphore_signal(
             barrier, inc=1, device_id=(r, along(z, u, planes, ahead)), device_id_type=MESH
         )
@@ -145,7 +145,7 @@
     land, (
         sound_land, sound_outbox,
         fetch_sems, region_sems, export_sems, along_send, along_recv, across_sems, own_sem,
-        sound_sems,
+        sound_sems, own_s, list_sem,
     ) = rest[: planes - 1], rest[planes - 1 :]
     wait_for_all = greet(regions, planes)
     fetches = [
@@ -190,6 +190,8 @@
         send_along(planes, ahead, cells, land[i], along_send.at[i], along_recv.at[i])
         for i, ahead in enumerate(ORDER)
     ]
+    own_list = pltpu.make_async_copy(exports.at[pl.ds(0, 1)], own_s, list_sem)
+    own_list.start()
     for copy in lists + calls + blocks[:2] + list(regionals) + blocks[2:]:
         copy.start()
 
@@ -231,7 +233,7 @@
         second = inverse * inverse
         for at, value in (
             (X, x), (Y, y), (Z, z), (INVERSE, inverse), (VX, vx), (VY, vy), (VZ, vz),
-            (SECOND, second), (THIRD, second * inverse), (SMALL, 0.05 * h),
+            (SECOND, second), (THIRD, 0.5 * second * inverse), (SMALL, 0.05 * h),
             (SOUND, SOUND_UNIT * jnp.sqrt(ADIABATIC * (ADIABATIC - 1.0) * e)),
             (HEAT, (ADIABATIC - 1.0) * e),
         ):
@@ -239,6 +241,8 @@
 
     for k in range(EARLY):
         compact(k)
+    own_list.wait()
+    choose(0, own_s, cells, outbox)
     drained = exports.at[pl.ds(1, planes - 1)]
     pltpu.make_async_copy(drained, drained, export_sems.at[1]).wait()
     pltpu.make_async_copy(drained, drained, export_sems.at[0]).wait()
@@ -250,7 +254,6 @@
     for slot in range(planes):
         choose(slot, exports_s, sound_land.at[slot], sound_outbox)
     send_across(0, planes, planes, sound_outbox, sounds, sound_sems.at[2], sound_sems.at[3])
-    choose(0, exports_s, cells, outbox)
     for i in range(planes - 1):
         if i + EARLY < C_DEV:
             compact(i + EARLY)
@@ -352,7 +355,7 @@
         inverse = 1.0 / h
         second = inverse * inverse
         derived[s, 0:1] = second
-        derived[s, 1:2] = second * inverse
+        derived[s, 1:2] = 0.5 * second * inverse
         derived[s, 2:3] = 0.05 * h
         derived[s, 3:4] = m * (1.5 / math.pi)
         sound = sounds[s]
@@ -536,14 +539,15 @@
                     square = jnp.maximum(dx * dx + dy * dy + dz * dz, TINY)
                     over = lax.rsqrt(square)
                     radius = square * over
-                    reach = radius * third
-                    outer = jnp.maximum(second - 0.5 * reach, 0.0)
-                    inner = jnp.maximum(second - reach, 0.0)
+                    half = radius * third
+                    outer = second - half
+                    inner = jnp.maximum(outer - half, 0.0)
+                    outer = jnp.maximum(outer, 0.0)
                     slope = outer * outer - inner * inner
-                    second_j = more[n, 0:1]
-                    reach = radius * more[n, 1:2]
-                    outer = jnp.maximum(second_j - 0.5 * reach, 0.0)
-                    inner = jnp.maximum(second_j - reach, 0.0)
+                    half = radius * more[n, 1:2]
+                    outer = more[n, 0:1] - half
+                    inner = jnp.maximum(outer - half, 0.0)
+                    outer = jnp.maximum(outer, 0.0)
                     slope += outer * outer - inner * inner
                     approach = (
                         (vx - near[n, 5:6]) * dx
@@ -612,7 +616,7 @@
             *[floats(C_DEV, 8, CAP) for _ in range(planes - 1)],
             floats(planes, C_DEV, 1, CAP), floats(PLANE, 2 * planes, 1, CAP),
             dma((11,)), dma((8,)), dma((2,)), dma((planes - 1,)), dma((planes - 1,)), dma((2,)),
-            dma, dma((4,)),
+            dma, dma((4,)), pltpu.SMEM((1, 2, planes * PLANE), jnp.int32), dma,
         ],
         compiler_params=pltpu.CompilerParams(
             collective_id=0, has_side_effects=True, vmem_limit_bytes=limit

time: 50.4 us -> 51 us (1.012)
  the two profiles are of different devices: /device:TPU:57 before, /device:TPU:48 now
where the time goes in v6:
time: 51 us; the launch traced here: 50.7 us
  Pallas kernels  50 us (98%)
  between operations  0.68 us (1%)
    pallas_call x1, Pallas kernels, shards(): pl.pallas_call(functools.partial(static_kernel, regions, planes), out_sha...  25.2 us
    pallas_call x1, Pallas kernels, shards(): pl.pallas_call(functools.partial(moving_kernel, regions, planes), out_sha...  11.6 us
    pallas_call x1, Pallas kernels, shards(): pl.pallas_call(force_kernel, out_shape=[shape(3, C_DEV, CAP), shape(3, C_...  8.69 us
    pallas_call x1, Pallas kernels, shards(): pl.pallas_call(density_kernel, out_shape=[shape(C_DEV, CAP), shape(2, C_D...  4.59 us

profile of v6, /device:TPU:48, one launch (start us, length us, event | category | flops | bytes accessed | tf_op | source)
XLA Modules:
  0.0 50.7 jit_solution(17259624294543660082)
XLA Ops:
  0.6 0.0 copy-start
  0.6 0.0 copy-start.1
  0.7 25.2 %shard_map.139 = (f32[138,8,128]{2,1,0:T(8,128)S(1)}, f32[138,1,128]{2,1,0:T(1,128)S(1)}, f32[12,8,128,128]{3,2,1,0:T(8,128)S(1)}, f32[8,128]{1,0:T(8,128)S(1)},...) custom-call(f32[3,8,128]{2,1,0:T(8,128)} %position.1, f32[3,8,128]{2,1,0:T(8,128)} %velocity.3, ...), custom_call_target="tpu_custom_call" | custom-call | tf_op jit(solution)/shard_map/pallas_call | solution.py:600
  25.9 4.6 %shard_map.140 = (f32[8,128]{1,0:T(8,128)S(1)}, f32[2,8,128,128]{3,2,1,0:T(8,128)S(1)}) custom-call(s32[8,128]{1,0:T(8,128)S(1)} %get-tuple-element.17.plan, f32[138,8,128]{2,1,0:T(8,128)S(1)} %get-tuple-element.19.table.sources, f32[12,8,128,128]{3,2,1,0:T(8,128)S(1)} %get-tuple-element.20.targets, f32[8,128]{1,0:T(8,128)S(1)} %get-tuple-element.21.rank, ...), custom_call_target="tpu_custom_call" | custom-call | tf_op jit(solution)/shard_map/pallas_call | solution.py:633
  30.5 11.6 %shard_map.141 = (f32[138,8,128]{2,1,0:T(8,128)S(1)}, s32[8,128]{1,0:T(8,128)S(1)}) custom-call(s32[8,2,64]{2,1,0:T(2,128)S(1)} %get-tuple-element.18.exports, f32[8,128]{1,0:T(8,128)S(1)} %get-tuple-element.23.density.density_in, f32[138,8,128]{2,1,0:T(8,128)S(1)} %get-tuple-element.19.table.sources, f32[138,1,128]{2,1,0:T(1,128)S(1)} %get-tuple-element.24.sounds, ...), custom_call_target="tpu_custom_call" | custom-call | tf_op jit(solution)/shard_map/pallas_call | solution.py:643
  42.0 0.0 copy-done
  42.0 0.0 copy-done.1
  42.0 8.7 %shard_map.142 = (f32[3,8,128]{2,1,0:T(8,128)}, f32[3,8,128]{2,1,0:T(8,128)}, f32[8,128]{1,0:T(8,128)}) custom-call(s32[8,128]{1,0:T(8,128)S(1)} %get-tuple-element.17.plan, s32[8,128]{1,0:T(8,128)S(1)} %get-tuple-element.25.offsets, f32[138,8,128]{2,1,0:T(8,128)S(1)} %get-tuple-element.19.table.sources, f32[138,8,128]{2,1,0:T(8,128)S(1)} %get-tuple-element.26.derived, ...), custom_call_target="tpu_custom_call" | custom-call | tf_op jit(solution)/shard_map/pallas_call | solution.py:656
Async XLA Ops:
  0.6 41.4 %copy-start = (f32[3,8,128]{2,1,0:T(8,128)S(1)}, f32[3,8,128]{2,1,0:T(8,128)}, u32[]{:S(2)}) copy-start(f32[3,8,128]{2,1,0:T(8,128)} %velocity.3) | copy-start | bytes 36868
  0.6 41.4 %copy-start.1 = (s32[8,128]{1,0:T(8,128)S(1)}, s32[8,128]{1,0:T(8,128)}, u32[]{:S(2)}) copy-start(s32[8,128]{1,0:T(8,128)} %time_bin.1) | copy-start | bytes 12292

commit v7 on v6

--- a/solution.py
+++ b/solution.py
@@ -96,7 +96,7 @@
     r, z, u = place()
     rows = 2 * slots
 
-    def send(ahead, carry):
+    for ahead in (4, 3, 5, 2, 6, 1, 7):
         to = lax.rem(u + ahead, PLANE)
         pltpu.make_async_remote_copy(
             src_ref=outbox.at[to, pl.ds(2 * first, rows)],
@@ -104,9 +104,6 @@
             send_sem=send_sem, recv_sem=recv_sem,
             device_id=(r, z * PLANE + to), device_id_type=MESH,
         ).start()
-        return carry
-
-    lax.fori_loop(1, PLANE, send, 0)
 
 
 def choose(slot, export, cells, outbox):

time: 51 us -> 52.3 us (1.025)
  the two profiles are of different devices: /device:TPU:48 before, /device:TPU:34 now
where the time goes in v7:
time: 52.3 us; the launch traced here: 52.7 us
  Pallas kernels  52 us (99%)
  between operations  0.68 us (1%)
    pallas_call x1, Pallas kernels, shards(): pl.pallas_call(functools.partial(static_kernel, regions, planes), out_sha...  24 us
    pallas_call x1, Pallas kernels, shards(): pl.pallas_call(functools.partial(moving_kernel, regions, planes), out_sha...  11.6 us
    pallas_call x1, Pallas kernels, shards(): pl.pallas_call(force_kernel, out_shape=[shape(3, C_DEV, CAP), shape(3, C_...  11 us
    pallas_call x1, Pallas kernels, shards(): pl.pallas_call(density_kernel, out_shape=[shape(C_DEV, CAP), shape(2, C_D...  5.48 us

profile of v7, /device:TPU:34, one launch (start us, length us, event | category | flops | bytes accessed | tf_op | source)
XLA Modules:
  0.0 52.7 jit_solution(6319903284976687491)
XLA Ops:
  0.6 0.0 copy-start
  0.6 0.0 copy-start.1
  0.7 24.0 %shard_map.139 = (f32[138,8,128]{2,1,0:T(8,128)S(1)}, f32[138,1,128]{2,1,0:T(1,128)S(1)}, f32[12,8,128,128]{3,2,1,0:T(8,128)S(1)}, f32[8,128]{1,0:T(8,128)S(1)},...) custom-call(f32[3,8,128]{2,1,0:T(8,128)} %position.1, f32[3,8,128]{2,1,0:T(8,128)} %velocity.3, ...), custom_call_target="tpu_custom_call" | custom-call | tf_op jit(solution)/shard_map/pallas_call | solution.py:597
  24.7 5.5 %shard_map.140 = (f32[8,128]{1,0:T(8,128)S(1)}, f32[2,8,128,128]{3,2,1,0:T(8,128)S(1)}) custom-call(s32[8,128]{1,0:T(8,128)S(1)} %get-tuple-element.17.plan, f32[138,8,128]{2,1,0:T(8,128)S(1)} %get-tuple-element.19.table.sources, f32[12,8,128,128]{3,2,1,0:T(8,128)S(1)} %get-tuple-element.20.targets, f32[8,128]{1,0:T(8,128)S(1)} %get-tuple-element.21.rank, ...), custom_call_target="tpu_custom_call" | custom-call | tf_op jit(solution)/shard_map/pallas_call | solution.py:630
  30.2 11.6 %shard_map.141 = (f32[138,8,128]{2,1,0:T(8,128)S(1)}, s32[8,128]{1,0:T(8,128)S(1)}) custom-call(s32[8,2,64]{2,1,0:T(2,128)S(1)} %get-tuple-element.18.exports, f32[8,128]{1,0:T(8,128)S(1)} %get-tuple-element.23.density.density_in, f32[138,8,128]{2,1,0:T(8,128)S(1)} %get-tuple-element.19.table.sources, f32[138,1,128]{2,1,0:T(1,128)S(1)} %get-tuple-element.24.sounds, ...), custom_call_target="tpu_custom_call" | custom-call | tf_op jit(solution)/shard_map/pallas_call | solution.py:640
  41.7 0.0 copy-done
  41.7 0.0 copy-done.1
  41.8 11.0 %shard_map.142 = (f32[3,8,128]{2,1,0:T(8,128)}, f32[3,8,128]{2,1,0:T(8,128)}, f32[8,128]{1,0:T(8,128)}) custom-call(s32[8,128]{1,0:T(8,128)S(1)} %get-tuple-element.17.plan, s32[8,128]{1,0:T(8,128)S(1)} %get-tuple-element.25.offsets, f32[138,8,128]{2,1,0:T(8,128)S(1)} %get-tuple-element.19.table.sources, f32[138,8,128]{2,1,0:T(8,128)S(1)} %get-tuple-element.26.derived, ...), custom_call_target="tpu_custom_call" | custom-call | tf_op jit(solution)/shard_map/pallas_call | solution.py:653
Async XLA Ops:
  0.6 41.1 %copy-start = (f32[3,8,128]{2,1,0:T(8,128)S(1)}, f32[3,8,128]{2,1,0:T(8,128)}, u32[]{:S(2)}) copy-start(f32[3,8,128]{2,1,0:T(8,128)} %velocity.3) | copy-start | bytes 36868
  0.6 41.1 %copy-start.1 = (s32[8,128]{1,0:T(8,128)S(1)}, s32[8,128]{1,0:T(8,128)}, u32[]{:S(2)}) copy-start(s32[8,128]{1,0:T(8,128)} %time_bin.1) | copy-start | bytes 12292

commit v8 on v7

--- a/solution.py
+++ b/solution.py
@@ -189,7 +189,17 @@
     ]
     own_list = pltpu.make_async_copy(exports.at[pl.ds(0, 1)], own_s, list_sem)
     own_list.start()
-    for copy in lists + calls + blocks[:2] + list(regionals) + blocks[2:]:
+    for copy in lists + calls:
+        copy.start()
+    first_core = lax.rem(lax.axis_index("cell"), 2) == 0
+
+    def start_blocks(order):
+        for ahead in order:
+            blocks[ORDER.index(ahead)].start()
+
+    pl.when(first_core)(lambda: start_blocks(ORDER))
+    pl.when(jnp.logical_not(first_core))(lambda: start_blocks([planes - a for a in ORDER]))
+    for copy in regionals:
         copy.start()
 
     live = active_v[...] > 0

time: 52.3 us -> 51.4 us (0.983)
  the two profiles are of different devices: /device:TPU:34 before, /device:TPU:57 now
where the time goes in v8:
time: 51.4 us
  Pallas kernels  50.7 us (99%)
  between operations  0.68 us (1%)
    pallas_call x1, Pallas kernels, shards(): pl.pallas_call(functools.partial(static_kernel, regions, planes), out_sha...  25.1 us
    pallas_call x1, Pallas kernels, shards(): pl.pallas_call(functools.partial(moving_kernel, regions, planes), out_sha...  11.5 us
    pallas_call x1, Pallas kernels, shards(): pl.pallas_call(force_kernel, out_shape=[shape(3, C_DEV, CAP), shape(3, C_...  9.28 us
    pallas_call x1, Pallas kernels, shards(): pl.pallas_call(density_kernel, out_shape=[shape(C_DEV, CAP), shape(2, C_D...  4.79 us

profile of v8, /device:TPU:57, one launch (start us, length us, event | category | flops | bytes accessed | tf_op | source)
XLA Modules:
  0.0 51.4 jit_solution(183888759228338168)
XLA Ops:
  0.6 0.0 copy-start
  0.6 0.0 copy-start.1
  0.7 25.1 %shard_map.139 = (f32[138,8,128]{2,1,0:T(8,128)S(1)}, f32[138,1,128]{2,1,0:T(1,128)S(1)}, f32[12,8,128,128]{3,2,1,0:T(8,128)S(1)}, f32[8,128]{1,0:T(8,128)S(1)},...) custom-call(f32[3,8,128]{2,1,0:T(8,128)} %position.1, f32[3,8,128]{2,1,0:T(8,128)} %velocity.3, ...), custom_call_target="tpu_custom_call" | custom-call | tf_op jit(solution)/shard_map/pallas_call | solution.py:607
  25.8 4.8 %shard_map.140 = (f32[8,128]{1,0:T(8,128)S(1)}, f32[2,8,128,128]{3,2,1,0:T(8,128)S(1)}) custom-call(s32[8,128]{1,0:T(8,128)S(1)} %get-tuple-element.17.plan, f32[138,8,128]{2,1,0:T(8,128)S(1)} %get-tuple-element.19.table.sources, f32[12,8,128,128]{3,2,1,0:T(8,128)S(1)} %get-tuple-element.20.targets, f32[8,128]{1,0:T(8,128)S(1)} %get-tuple-element.21.rank, ...), custom_call_target="tpu_custom_call" | custom-call | tf_op jit(solution)/shard_map/pallas_call | solution.py:640
  30.6 11.5 %shard_map.141 = (f32[138,8,128]{2,1,0:T(8,128)S(1)}, s32[8,128]{1,0:T(8,128)S(1)}) custom-call(s32[8,2,64]{2,1,0:T(2,128)S(1)} %get-tuple-element.18.exports, f32[8,128]{1,0:T(8,128)S(1)} %get-tuple-element.23.density.density_in, f32[138,8,128]{2,1,0:T(8,128)S(1)} %get-tuple-element.19.table.sources, f32[138,1,128]{2,1,0:T(1,128)S(1)} %get-tuple-element.24.sounds, ...), custom_call_target="tpu_custom_call" | custom-call | tf_op jit(solution)/shard_map/pallas_call | solution.py:650
  42.1 0.0 copy-done
  42.1 0.0 copy-done.1
  42.1 9.3 %shard_map.142 = (f32[3,8,128]{2,1,0:T(8,128)}, f32[3,8,128]{2,1,0:T(8,128)}, f32[8,128]{1,0:T(8,128)}) custom-call(s32[8,128]{1,0:T(8,128)S(1)} %get-tuple-element.17.plan, s32[8,128]{1,0:T(8,128)S(1)} %get-tuple-element.25.offsets, f32[138,8,128]{2,1,0:T(8,128)S(1)} %get-tuple-element.19.table.sources, f32[138,8,128]{2,1,0:T(8,128)S(1)} %get-tuple-element.26.derived, ...), custom_call_target="tpu_custom_call" | custom-call | tf_op jit(solution)/shard_map/pallas_call | solution.py:663
Async XLA Ops:
  0.6 41.5 %copy-start = (f32[3,8,128]{2,1,0:T(8,128)S(1)}, f32[3,8,128]{2,1,0:T(8,128)}, u32[]{:S(2)}) copy-start(f32[3,8,128]{2,1,0:T(8,128)} %velocity.3) | copy-start | bytes 36868
  0.6 41.5 %copy-start.1 = (s32[8,128]{1,0:T(8,128)S(1)}, s32[8,128]{1,0:T(8,128)}, u32[]{:S(2)}) copy-start(s32[8,128]{1,0:T(8,128)} %time_bin.1) | copy-start | bytes 12292
